TPU v7x, 32 devices: a whole 2x2x4 slice. The times are simulated.
32 devices in a mesh: dp: 16 (over z, y, x), tensor: 2 (over core).
Axes of the slice: x: 2, y: 2, z: 4, core: 2. Of those that a mesh axis runs over, the one named last changes fastest.
Arguments:
- tokens: bfloat16 [4096, 2048], P(('dp', 'tensor')), may hold values from -6 to 6
- norm1_gain: bfloat16 [2048], P('dp'), may hold values from 0.099609375 to 1.8984375
- qkv_weight: bfloat16 [2048, 3, 2048], P('dp', None, 'tensor'), may hold values from -0.125 to 0.125
- out_weight: bfloat16 [2048, 2048], P('dp', 'tensor'), may hold values from -0.5 to 0.5
- norm2_gain: bfloat16 [2048], P('dp'), may hold values from 0.099609375 to 1.8984375
- gate_up_weight: bfloat16 [2048, 2, 5632], P('dp', None, 'tensor'), may hold values from -0.125 to 0.125
- down_weight: bfloat16 [2048, 5632], P('dp', 'tensor'), may hold values from -0.078125 to 0.078125
- doc_lengths: int32 [16, 8], P('dp'), may hold values from 1 to 128, 256 in all within a row
- cotangent: bfloat16 [4096, 2048], P(('dp', 'tensor')), may hold values from -6 to 6
Outputs:
- output: bfloat16 [4096, 2048], P(('dp', 'tensor'))
- input_grad: bfloat16 [4096, 2048], P(('dp', 'tensor'))
- norm1_gain_grad: float32 [2048], P('dp')
- qkv_grad: float32 [2048, 3, 2048], P('dp', None, 'tensor')
- out_grad: float32 [2048, 2048], P('dp', 'tensor')
- norm2_gain_grad: float32 [2048], P('dp')
- gate_up_grad: float32 [2048, 2, 5632], P('dp', None, 'tensor')
- down_grad: float32 [2048, 5632], P('dp', 'tensor')
Inputs may be any that keep to these rules, and one draw needn't show every extreme that they name: `doc_lengths`: in every packed row the 8 lengths sum to 256, and the longest is 128.
All inputs are finite; a program needn't handle non-finite values.
Results may differ from a plain program's by a relative error of at most 0.014.
Values may be sent and summed in bfloat16 or wider, within the bound.
No kernel may reach another device: no remote copies, remote signals or barrier semaphores. Data moves between devices by JAX's collectives and lax.ppermute only.
A program may use at most 256 MiB of HBM per device.

v0:
```python
import math

import jax
import jax.numpy as jnp
from jax import lax
from jax.sharding import PartitionSpec as P

HEAD_DIM = 128


EPS_NORM = 1e-05
MASKED_SCORE = -1e30


def doc_layout(lengths_row, row_count):
    ends_at = jnp.cumsum(lengths_row, dtype=jnp.int32)
    positions = jnp.arange(row_count, dtype=jnp.int32)
    passed = positions[:, None] >= ends_at[None, :]
    segment = jnp.sum(passed.astype(jnp.int32), axis=1, dtype=jnp.int32)
    doc_start = jnp.sum(jnp.where(passed, lengths_row[None, :], 0), axis=1, dtype=jnp.int32)
    offset = (positions - doc_start).astype(jnp.float32)
    allowed = (segment[:, None] == segment[None, :]) & (positions[:, None] >= positions[None, :])
    half_dim = HEAD_DIM // 2
    inverse = jnp.exp(
        jnp.arange(half_dim, dtype=jnp.float32) * (-2.0 * math.log(10000.0) / HEAD_DIM)
    )
    angles = offset[:, None] * inverse[None, :]
    return (allowed, jnp.cos(angles), jnp.sin(angles))


def rotate(values, cosine, sine_part, sign):
    half_dim = values.shape[-1] // 2
    first_half = values[..., :half_dim]
    second = values[..., half_dim:]
    cos_wide = cosine[:, None, :]
    sin_wide = sign * sine_part[:, None, :]
    return jnp.concatenate(
        [first_half * cos_wide - second * sin_wide, second * cos_wide + first_half * sin_wide],
        axis=-1,
    )


def rms_scale(values):
    return lax.rsqrt(jnp.mean(values * values, axis=-1, keepdims=True) + EPS_NORM)


def norm_back(grad_in, normed, scaling, gain_f32):
    gain_part = jnp.sum(grad_in * normed, axis=0)
    grad_normed = grad_in * gain_f32
    return (
        scaling * (grad_normed - normed * jnp.mean(grad_normed * normed, axis=-1, keepdims=True)),
        gain_part,
    )


def contract_rows(left, right):
    return lax.dot_general(
        left, right, (((0,), (0,)), ((), ())), preferred_element_type=jnp.float32
    )


def contract_last(left, right):
    return lax.dot_general(
        left, right, (((1,), (1,)), ((), ())), preferred_element_type=jnp.float32
    )


def head_scores(queries, keys_head, allowed, scaling):
    scores = contract_last(queries, keys_head) * scaling
    return jnp.where(allowed, scores, MASKED_SCORE)


def head_forward(pieces, allowed, scaling):
    queries, keys_head, values_head = pieces
    scores = head_scores(queries, keys_head, allowed, scaling)
    row_max = jnp.max(scores, axis=1, keepdims=True)
    exp_scores = jnp.exp(scores - row_max)
    row_total = jnp.sum(exp_scores, axis=1, keepdims=True)
    weights = (exp_scores / row_total).astype(jnp.bfloat16)
    mixed = jnp.dot(weights, values_head, preferred_element_type=jnp.float32).astype(jnp.bfloat16)
    return (mixed, (row_max + jnp.log(row_total))[:, 0])


def head_backward(pieces, allowed, scaling):
    queries, keys_head, values_head, grad_mixed, log_total = pieces
    scores = head_scores(queries, keys_head, allowed, scaling)
    probs = jnp.exp(scores - log_total[:, None])
    grad_values = contract_rows(probs.astype(jnp.bfloat16), grad_mixed).astype(jnp.bfloat16)
    grad_probs = contract_last(grad_mixed, values_head)
    delta_sum = jnp.sum(probs * grad_probs, axis=1, keepdims=True)
    grad_scores = (probs * (grad_probs - delta_sum) * scaling).astype(jnp.bfloat16)
    grad_queries = jnp.dot(grad_scores, keys_head, preferred_element_type=jnp.float32)
    grad_keys = contract_rows(grad_scores, queries)
    return (grad_queries, grad_keys, grad_values)


def shards(
    tokens,
    norm1_gain,
    qkv_weight,
    out_weight,
    norm2_gain,
    gate_up_weight,
    down_weight,
    doc_lengths,
    cotangent,
):
    row_dev = tokens.shape[0]
    row_count = row_dev * lax.axis_size("tensor")
    local_width = qkv_weight.shape[2]
    hidden_width = gate_up_weight.shape[2]
    heads_here = local_width // HEAD_DIM
    scaling = HEAD_DIM ** (-0.5)
    shape3 = (row_count, heads_here, HEAD_DIM)
    qkv_full, out_full, gain_one = (
        lax.all_gather(qkv_weight, "dp", axis=0, tiled=True),
        lax.all_gather(out_weight, "dp", axis=0, tiled=True),
        lax.all_gather(norm1_gain, "dp", axis=0, tiled=True),
    )
    gate_up_full, down_full, gain_two = (
        lax.all_gather(gate_up_weight, "dp", axis=0, tiled=True),
        lax.all_gather(down_weight, "dp", axis=0, tiled=True),
        lax.all_gather(norm2_gain, "dp", axis=0, tiled=True),
    )
    qkv_mat = qkv_full.reshape(qkv_full.shape[0], 3 * local_width)
    gate_up_mat = gate_up_full.reshape(gate_up_full.shape[0], 2 * hidden_width)
    gain_one = gain_one.astype(jnp.float32)
    gain_two = gain_two.astype(jnp.float32)
    allowed, cosine, sine_part = doc_layout(doc_lengths[0], row_count)
    residual = tokens.astype(jnp.float32)
    scale_one = rms_scale(residual)
    normed_one = residual * scale_one
    norm_out_one = (normed_one * gain_one).astype(jnp.bfloat16)
    rows_one = lax.all_gather(norm_out_one, "tensor", axis=0, tiled=True)
    projected = jnp.dot(rows_one, qkv_mat, preferred_element_type=jnp.float32)
    queries = rotate(projected[:, :local_width].reshape(shape3), cosine, sine_part, 1.0).astype(
        jnp.bfloat16
    )
    keys_rot = rotate(
        projected[:, local_width : 2 * local_width].reshape(shape3), cosine, sine_part, 1.0
    ).astype(jnp.bfloat16)
    values_all = projected[:, 2 * local_width :].reshape(shape3).astype(jnp.bfloat16)
    query_heads = jnp.swapaxes(queries, 0, 1)
    key_heads = jnp.swapaxes(keys_rot, 0, 1)
    value_heads = jnp.swapaxes(values_all, 0, 1)
    mixed_heads, log_totals = lax.map(
        lambda pieces: head_forward(pieces, allowed, scaling), (query_heads, key_heads, value_heads)
    )
    mixed_flat = jnp.swapaxes(mixed_heads, 0, 1).reshape(row_count, local_width)
    attn = lax.psum_scatter(
        contract_last(mixed_flat, out_full), "tensor", scatter_dimension=0, tiled=True
    )
    stream = residual + attn
    scale_two = rms_scale(stream)
    normed_two = stream * scale_two
    norm_out_two = (normed_two * gain_two).astype(jnp.bfloat16)
    rows_two = lax.all_gather(norm_out_two, "tensor", axis=0, tiled=True)
    gate_up = jnp.dot(rows_two, gate_up_mat, preferred_element_type=jnp.float32)
    gate = gate_up[:, :hidden_width]
    upper = gate_up[:, hidden_width:]
    sigma = jax.nn.sigmoid(gate)
    silu_gate = gate * sigma
    hidden = (silu_gate * upper).astype(jnp.bfloat16)
    mlp_out = lax.psum_scatter(
        contract_last(hidden, down_full).astype(jnp.bfloat16),
        "tensor",
        scatter_dimension=0,
        tiled=True,
    ).astype(jnp.float32)
    output = (stream + mlp_out).astype(jnp.bfloat16)
    cot_rows = lax.all_gather(cotangent, "tensor", axis=0, tiled=True)
    down_part = contract_rows(cot_rows, hidden)
    grad_hidden = jnp.dot(cot_rows, down_full, preferred_element_type=jnp.float32)
    grad_gate = (grad_hidden * upper * (sigma * (1.0 + gate * (1.0 - sigma)))).astype(jnp.bfloat16)
    grad_upper = (grad_hidden * silu_gate).astype(jnp.bfloat16)
    grad_gate_up = jnp.concatenate([grad_gate, grad_upper], axis=1)
    gate_up_part = contract_rows(rows_two, grad_gate_up)
    grad_norm_two = lax.psum_scatter(
        contract_last(grad_gate_up, gate_up_mat), "tensor", scatter_dimension=0, tiled=True
    )
    grad_from_two, gain_two_part = norm_back(grad_norm_two, normed_two, scale_two, gain_two)
    grad_stream = cotangent.astype(jnp.float32) + grad_from_two
    stream_rows = lax.all_gather(grad_stream.astype(jnp.bfloat16), "tensor", axis=0, tiled=True)
    out_part = contract_rows(stream_rows, mixed_flat)
    grad_mixed = jnp.dot(stream_rows, out_full, preferred_element_type=jnp.float32).astype(
        jnp.bfloat16
    )
    grad_mixed_heads = jnp.swapaxes(grad_mixed.reshape(shape3), 0, 1)
    grad_q_heads, grad_k_heads, grad_v_heads = lax.map(
        lambda pieces: head_backward(pieces, allowed, scaling),
        (query_heads, key_heads, value_heads, grad_mixed_heads, log_totals),
    )
    grad_queries = (
        rotate(jnp.swapaxes(grad_q_heads, 0, 1), cosine, sine_part, -1.0)
        .reshape(row_count, local_width)
        .astype(jnp.bfloat16)
    )
    grad_keys = (
        rotate(jnp.swapaxes(grad_k_heads, 0, 1), cosine, sine_part, -1.0)
        .reshape(row_count, local_width)
        .astype(jnp.bfloat16)
    )
    grad_values = jnp.swapaxes(grad_v_heads, 0, 1).reshape(row_count, local_width)
    grad_qkv = jnp.concatenate([grad_queries, grad_keys, grad_values], axis=1)
    qkv_part = contract_rows(rows_one, grad_qkv)
    grad_norm_one = lax.psum_scatter(
        contract_last(grad_qkv, qkv_mat), "tensor", scatter_dimension=0, tiled=True
    )
    grad_from_one, gain_one_part = norm_back(grad_norm_one, normed_one, scale_one, gain_one)
    input_grad = (grad_stream + grad_from_one).astype(jnp.bfloat16)
    qkv_flat, out_grad, gain_one_sum, gate_up_flat, down_grad, gain_two_sum = (
        lax.psum_scatter(qkv_part, "dp", scatter_dimension=0, tiled=True),
        lax.psum_scatter(out_part, "dp", scatter_dimension=0, tiled=True),
        lax.psum_scatter(gain_one_part, "dp", scatter_dimension=0, tiled=True),
        lax.psum_scatter(gate_up_part, "dp", scatter_dimension=0, tiled=True),
        lax.psum_scatter(down_part, "dp", scatter_dimension=0, tiled=True),
        lax.psum_scatter(gain_two_part, "dp", scatter_dimension=0, tiled=True),
    )
    qkv_grad = qkv_flat.reshape(qkv_flat.shape[0], 3, local_width)
    gate_up_grad = gate_up_flat.reshape(gate_up_flat.shape[0], 2, hidden_width)
    gain_one_grad, gain_two_grad = lax.psum((gain_one_sum, gain_two_sum), "tensor")
    return (
        output,
        input_grad,
        gain_one_grad,
        qkv_grad,
        out_grad,
        gain_two_grad,
        gate_up_grad,
        down_grad,
    )


def solution(mesh):
    placed = (
        P(("dp", "tensor"), None),
        P("dp"),
        P("dp", None, "tensor"),
        P("dp", "tensor"),
        P("dp"),
        P("dp", None, "tensor"),
        P("dp", "tensor"),
        P("dp", None),
        P(("dp", "tensor"), None),
    )
    return jax.shard_map(
        shards,
        mesh=mesh,
        in_specs=placed,
        out_specs=(
            P(("dp", "tensor"), None),
            P(("dp", "tensor"), None),
            P("dp"),
            P("dp", None, "tensor"),
            P("dp", "tensor"),
            P("dp"),
            P("dp", None, "tensor"),
            P("dp", "tensor"),
        ),
        check_vma=False,
    )
```

profile of v0, /device:TPU:24, one launch (start us, length us, event | category | flops | bytes accessed | tf_op | source)
XLA Modules:
  0.0 2903.7 jit_solution(9608922477505706491)
XLA Ops:
  7.2 32.5 %all-gather = bf16[16,1,128]{2,1,0:T(2,128)(2,1)S(1)} all-gather(bf16[1,1,128]{2,1,0:T(2,128)(2,1)} %bitcast.180), channel_id=1, replica_groups=mesh['dp'=16,'tensor'=2] {'dp'}, dimensions={0}, use_global_device_ids=true | all-gather | bytes 4352 | tf_op jit(solution)/shard_map/all_gather | solution.py:118
  46.8 9.7 all-gather.11.cloned.1.call-done
  56.5 198.3 %all-gather.13.cloned.1.call-done = bf16[2048,3,1024]{0,2,1:T(8,128)(2,1)} async-done(((bf16[128,3,1024]{0,2,1:T(8,128)(2,1)}), bf16[2048,3,1024]{0,2,1:T(8,128)(2,1)}) %all-gather.13.cloned.1.call-update) | async-done | bytes 12582928 | tf_op jit(solution)/shard_map/all_gather | solution.py:116
  272.4 60.0 %all-gather.15.cloned.1.call-done = bf16[2048,1024]{1,0:T(8,128)(2,1)} async-done(((bf16[128,1024]{1,0:T(8,128)(2,1)}), bf16[2048,1024]{1,0:T(8,128)(2,1)}) %all-gather.15.cloned.1.call-update) | async-done | bytes 4194320 | tf_op jit(solution)/shard_map/all_gather | solution.py:117
  337.9 31.9 %all-gather.1 = bf16[16,1,128]{2,1,0:T(2,128)(2,1)S(1)} all-gather(bf16[1,1,128]{2,1,0:T(2,128)(2,1)S(1)} %bitcast.181), channel_id=1, replica_groups=mesh['dp'=16,'tensor'=2] {'dp'}, dimensions={0}, use_global_device_ids=true | all-gather | bytes 4352 | tf_op jit(solution)/shard_map/all_gather | solution.py:123
  373.9 226.5 %all-gather.19.cloned.1.call-done = bf16[2048,2,2816]{2,1,0:T(2,128)(2,1)} async-done(((bf16[128,2,2816]{2,1,0:T(2,128)(2,1)}), bf16[2048,2,2816]{2,1,0:T(2,128)(2,1)}) %all-gather.19.cloned.1.call-update) | async-done | bytes 23068688 | tf_op jit(solution)/shard_map/all_gather | solution.py:121
  600.5 24.3 copy.97
  624.7 12.6 fusion.72
  637.3 130.8 %all-gather.21.cloned.1.call-done = bf16[2048,2816]{1,0:T(8,128)(2,1)} async-done(((bf16[128,2816]{1,0:T(8,128)(2,1)}), bf16[2048,2816]{1,0:T(8,128)(2,1)}) %all-gather.21.cloned.1.call-update) | async-done | bytes 11534352 | tf_op jit(solution)/shard_map/all_gather | solution.py:122
  768.1 11.5 multiply_convert_fusion.2
  779.6 12.5 fusion.46
  792.2 10.1 reduce-scatter.13.cloned.1.call-done
  806.5 10.1 all-gather.25.cloned.1.call-done
  822.1 59.6 %while.29 = (s32[]{:T(128)}, f32[8,256,128]{1,2,0:T(8,128)}, f32[8,256,128]{1,2,0:T(8,128)}, bf16[8,256,128]{1,2,0:T(8,128)(2,1)}, bf16[8,256,128]{2,1,0:T(8,128...) while((s32[]{:T(128)}, f32[8,256,128]{1,2,0:T(8,128)}, ...), condition=%wide.region_15.16_spmd.clone, body=%wide.region_13.15_spmd.clone.sunk | while | flops 84770560 | bytes 3026049 | solution.py:189
  884.6 11.5 fusion.61
  896.2 8.4 convolution_convert_fusion.2
  904.7 10.7 convolution_bitcast_fusion.2
  917.1 13.1 fusion.60
  931.3 19.8 fusion.45
  960.7 74.2 %all-reduce.2 = (f32[2048]{0:T(1024)S(1)}, f32[2048]{0:T(1024)S(1)}) all-reduce(f32[2048]{0:T(1024)S(1)} %get-tuple-element.230, f32[2048]{0:T(1024)S(1)} %get-tuple-element.228), channel_id=6, replica_groups=mesh['dp'=16,'tensor'=2] {'dp'}, use_global_device_ids=true, to_apply=%region_19.20.clone | all-reduce | flops 4096 | bytes 32768
  1040.8 358.7 %reduce-scatter.23.cloned.1.call-done = f32[128,2816]{0,1:T(8,128)} async-done(((f32[2048,2816]{0,1:T(8,128)}), f32[128,2816]{0,1:T(8,128)}) %reduce-scatter.23.cloned.1.call-update) | async-done | bytes 1441808 | tf_op jit(solution)/shard_map/reduce_scatter | solution.py:216
  1402.4 367.6 %reduce-scatter.17.cloned.1.call-done = f32[128,3072]{1,0:T(8,128)} async-done(((f32[2048,3072]{1,0:T(8,128)}), f32[128,3072]{1,0:T(8,128)}) %reduce-scatter.17.cloned.1.call-update) | async-done | bytes 1572880 | tf_op jit(solution)/shard_map/reduce_scatter | solution.py:212
  1773.6 937.8 %reduce-scatter.21.cloned.1.call-done = f32[128,5632]{1,0:T(8,128)} async-done(((f32[2048,5632]{1,0:T(8,128)}), f32[128,5632]{1,0:T(8,128)}) %reduce-scatter.21.cloned.1.call-update) | async-done | bytes 2883600 | tf_op jit(solution)/shard_map/reduce_scatter | solution.py:215
  2716.2 180.5 %reduce-scatter.19.cloned.1.call-done = f32[128,1024]{1,0:T(8,128)} async-done(((f32[2048,1024]{1,0:T(8,128)}), f32[128,1024]{1,0:T(8,128)}) %reduce-scatter.19.cloned.1.call-update) | async-done | bytes 524304 | tf_op jit(solution)/shard_map/reduce_scatter | solution.py:213
  (265 shorter events, 140.6 us)
Async XLA Ops:
  7.2 39.0 %copy-start.23 = (s32[1,8]{1,0:T(1,128)S(1)}, s32[1,8]{1,0:T(1,128)}, u32[]{:S(2)}) copy-start(s32[1,8]{1,0:T(1,128)} %param.20) | copy-start | bytes 100
  7.2 49.3 %all-gather.11.cloned.1.call-start = ((), (), s32[]{:S(2)}) async-start(), calls=%async_computation.8 | async-start | bytes 1572864 | tf_op jit(solution)/shard_map/all_gather | solution.py:134
  39.7 221.8 %copy-start.18 = (f32[16,1,128]{2,1,0:T(1,128)}, f32[16,1,128]{2,1,0:T(1,128)S(1)}, u32[]{:S(2)}) copy-start(f32[16,1,128]{2,1,0:T(1,128)S(1)} %convert_element_type.104) | copy-start | bytes 24580
  41.0 220.6 %copy-start.20 = (f32[128]{0:T(128)}, f32[128]{0:T(128)S(1)}, u32[]{:S(2)}) copy-start(f32[128]{0:T(128)S(1)} %add_rsqrt_fusion.1) | copy-start | bytes 1540
  43.0 211.8 %all-gather.13.cloned.1.call-start = ((), (), s32[]{:S(2)}) async-start(), calls=%async_computation.9 | async-start | bytes 13369344 | tf_op jit(solution)/shard_map/all_gather | solution.py:116
  45.4 287.0 %all-gather.15.cloned.1.call-start = ((), (), s32[]{:S(2)}) async-start(), calls=%async_computation.10 | async-start | bytes 4456448 | tf_op jit(solution)/shard_map/all_gather | solution.py:117
  46.1 323.6 %reduce-scatter.9.cloned.1.call-start = ((), (), s32[]{:S(2)}) async-start(), calls=%async_computation.11 | async-start | bytes 3145728 | tf_op jit(solution)/shard_map/reduce_scatter | solution.py:150
  272.3 60.0 %copy-start.15 = (bf16[8,256,128]{2,1,0:T(8,128)(2,1)}, bf16[8,256,128]{2,1,0:T(8,128)(2,1)S(1)}, u32[]{:S(2)}) copy-start(bf16[8,256,128]{2,1,0:T(8,128)(2,1)S(1)} %get-tuple-element.524) | copy-start | bytes 1572868
  272.4 64.8 %copy-start.11 = (bf16[8,256,128]{1,2,0:T(8,128)(2,1)}, bf16[8,256,128]{1,2,0:T(8,128)(2,1)S(1)}, u32[]{:S(2)}) copy-start(bf16[8,256,128]{1,2,0:T(8,128)(2,1)S(1)} %get-tuple-element.100) | copy-start | bytes 1572868
  272.4 64.8 %copy-start.16 = (bf16[8,256,128]{2,1,0:T(8,128)(2,1)}, bf16[8,256,128]{2,1,0:T(8,128)(2,1)S(1)}, u32[]{:S(2)}) copy-start(bf16[8,256,128]{2,1,0:T(8,128)(2,1)S(1)} %get-tuple-element.525) | copy-start | bytes 1572868
  272.4 64.8 %copy-start.17 = (bf16[8,256,128]{2,1,0:T(8,128)(2,1)}, bf16[8,256,128]{2,1,0:T(8,128)(2,1)S(1)}, u32[]{:S(2)}) copy-start(bf16[8,256,128]{2,1,0:T(8,128)(2,1)S(1)} %get-tuple-element.526) | copy-start | bytes 1572868
  337.2 263.2 %all-gather.19.cloned.1.call-start = ((), (), s32[]{:S(2)}) async-start(), calls=%async_computation.13 | async-start | bytes 24510464 | tf_op jit(solution)/shard_map/all_gather | solution.py:121
  337.8 286.9 %all-gather.17.cloned.1.call-start = ((), (), s32[]{:S(2)}) async-start(), calls=%async_computation.12 | async-start | bytes 1572864 | tf_op jit(solution)/shard_map/all_gather | solution.py:157
  372.2 265.1 %all-gather.23.cloned.1.call-start = ((), (), s32[]{:S(2)}) async-start(), calls=%async_computation.16 | async-start | bytes 1572864 | tf_op jit(solution)/shard_map/all_gather | solution.py:171
  373.0 395.1 %all-gather.21.cloned.1.call-start = ((), (), s32[]{:S(2)}) async-start(), calls=%async_computation.14 | async-start | bytes 12255232 | tf_op jit(solution)/shard_map/all_gather | solution.py:122
  373.7 428.6 %reduce-scatter.13.cloned.1.call-start = ((), (), s32[]{:S(2)}) async-start(), calls=%async_computation.17 | async-start | bytes 3145728 | tf_op jit(solution)/shard_map/reduce_scatter | solution.py:178
  792.2 24.4 all-gather.25.cloned.1.call-start
  806.3 152.8 %reduce-scatter.15.cloned.1.call-start = ((), (), s32[]{:S(2)}) async-start(), calls=%async_computation.19 | async-start | bytes 3145728 | tf_op jit(solution)/shard_map/reduce_scatter | solution.py:206
  896.1 141.9 %reduce-scatter.11.cloned.1.call-start = ((), (), s32[]{:S(2)}) async-start(), calls=%async_computation.15 | async-start | bytes 1572864 | tf_op jit(solution)/shard_map/reduce_scatter | solution.py:164
  904.6 494.9 %reduce-scatter.23.cloned.1.call-start = ((), (), s32[]{:S(2)}) async-start(), calls=%async_computation.23 | async-start | bytes 24510464 | tf_op jit(solution)/shard_map/reduce_scatter | solution.py:216
  915.4 854.6 %reduce-scatter.17.cloned.1.call-start = ((), (), s32[]{:S(2)}) async-start(), calls=%async_computation.20 | async-start | bytes 26738688 | tf_op jit(solution)/shard_map/reduce_scatter | solution.py:212
  930.1 1781.3 %reduce-scatter.21.cloned.1.call-start = ((), (), s32[]{:S(2)}) async-start(), calls=%async_computation.22 | async-start | bytes 49020928 | tf_op jit(solution)/shard_map/reduce_scatter | solution.py:215
  951.2 1945.6 %reduce-scatter.19.cloned.1.call-start = ((), (), s32[]{:S(2)}) async-start(), calls=%async_computation.21 | async-start | bytes 8912896 | tf_op jit(solution)/shard_map/reduce_scatter | solution.py:213
  957.2 80.8 %copy-start.2 = (f32[128,2048]{1,0:T(8,128)S(1)}, f32[128,2048]{1,0:T(8,128)}, u32[]{:S(2)}) copy-start(f32[128,2048]{1,0:T(8,128)} %reduce-scatter.13.cloned.1.call-done) | copy-start | bytes 3145732
  (17 other events, 65.5 us)
Sparse Core Ops, SparseCore 0:
  43.1 13.2 all-gather.10
  59.8 194.9 all-gather.12
  257.6 74.7 all-gather.14
  337.3 9.8 reduce-scatter.8
  350.2 250.2 all-gather.18
  602.5 9.3 all-gather.16
  613.6 10.1 all-gather.22
  626.9 141.1 all-gather.20
  792.3 9.9 reduce-scatter.12
  806.4 10.1 all-gather.24
  896.2 10.7 reduce-scatter.14
  909.2 9.6 reduce-scatter.10
  921.3 478.2 reduce-scatter.22
  1405.1 364.8 reduce-scatter.16
  1772.3 939.0 reduce-scatter.20
  2714.1 182.6 reduce-scatter.18
where the time goes:
time: 2920 us; the launch traced here: 2900 us
  waiting for transfers between devices  2490 us (85%)
  matrix products  177 us (6%)
  blocking collectives  141 us (5%)
  local copies, waits for them, and re-layouts  57.2 us (2%)
    reduce_scatter x1, waiting for transfers between devices, shards(): lax.psum_scatter(gate_up_part, 'dp', scatter_dimension=0, tiled=True)  938 us
    reduce_scatter x1, waiting for transfers between devices, shards(): lax.psum_scatter(qkv_part, 'dp', scatter_dimension=0, tiled=True)  368 us
    reduce_scatter x1, waiting for transfers between devices, shards(): lax.psum_scatter(down_part, 'dp', scatter_dimension=0, tiled=True)  359 us
    all_gather x1, waiting for transfers between devices, shards(): lax.all_gather(gate_up_weight, 'dp', axis=0, tiled=True)  227 us
    all_gather x1, waiting for transfers between devices, shards(): lax.all_gather(qkv_weight, 'dp', axis=0, tiled=True)  198 us
    reduce_scatter x1, waiting for transfers between devices, shards(): lax.psum_scatter(out_part, 'dp', scatter_dimension=0, tiled=True)  181 us
    all_gather x1, waiting for transfers between devices, shards(): lax.all_gather(down_weight, 'dp', axis=0, tiled=True)  131 us
    unnamed x1, blocking collectives  74.2 us
  transfers between devices with their start and end apart: 16, of which 11 were waited for; matrix products, arithmetic and copies ran while one was open for 5% of the time, Pallas kernels for 0%

commit v1 on v0

--- a/solution.py
+++ b/solution.py
@@ -13,7 +13,10 @@
 
 
 def doc_layout(lengths_row, row_count):
-    ends_at = jnp.cumsum(lengths_row, dtype=jnp.int32)
+    docs = jnp.arange(lengths_row.shape[0], dtype=jnp.int32)
+    ends_at = jnp.sum(
+        jnp.where(docs[None, :] <= docs[:, None], lengths_row[None, :], 0), axis=1, dtype=jnp.int32
+    )
     positions = jnp.arange(row_count, dtype=jnp.int32)
     passed = positions[:, None] >= ends_at[None, :]
     segment = jnp.sum(passed.astype(jnp.int32), axis=1, dtype=jnp.int32)

time: 2920 us -> 2920 us (level)
  no operation moved by 1% of the time
where the time goes in v1:
time: 2920 us; the launch traced here: 2900 us
  waiting for transfers between devices  2490 us (85%)
  matrix products  177 us (6%)
  blocking collectives  141 us (5%)
  local copies, waits for them, and re-layouts  57.2 us (2%)
    reduce_scatter x1, waiting for transfers between devices, shards(): lax.psum_scatter(gate_up_part, 'dp', scatter_dimension=0, tiled=True)  938 us
    reduce_scatter x1, waiting for transfers between devices, shards(): lax.psum_scatter(qkv_part, 'dp', scatter_dimension=0, tiled=True)  368 us
    reduce_scatter x1, waiting for transfers between devices, shards(): lax.psum_scatter(down_part, 'dp', scatter_dimension=0, tiled=True)  359 us
    all_gather x1, waiting for transfers between devices, shards(): lax.all_gather(gate_up_weight, 'dp', axis=0, tiled=True)  227 us
    all_gather x1, waiting for transfers between devices, shards(): lax.all_gather(qkv_weight, 'dp', axis=0, tiled=True)  198 us
    reduce_scatter x1, waiting for transfers between devices, shards(): lax.psum_scatter(out_part, 'dp', scatter_dimension=0, tiled=True)  181 us
    all_gather x1, waiting for transfers between devices, shards(): lax.all_gather(down_weight, 'dp', axis=0, tiled=True)  131 us
    unnamed x1, blocking collectives  74.2 us
  transfers between devices with their start and end apart: 16, of which 11 were waited for; matrix products, arithmetic and copies ran while one was open for 5% of the time, Pallas kernels for 0%

profile of v1, /device:TPU:24, one launch (start us, length us, event | category | flops | bytes accessed | tf_op | source)
XLA Modules:
  0.0 2903.7 jit_solution(16602350595223281510)
XLA Ops:
  7.2 32.5 %all-gather = bf16[16,1,128]{2,1,0:T(2,128)(2,1)S(1)} all-gather(bf16[1,1,128]{2,1,0:T(2,128)(2,1)} %bitcast.178), channel_id=1, replica_groups=mesh['dp'=16,'tensor'=2] {'dp'}, dimensions={0}, use_global_device_ids=true | all-gather | bytes 4352 | tf_op jit(solution)/shard_map/all_gather | solution.py:121
  46.7 9.8 all-gather.11.cloned.1.call-done
  56.5 198.3 %all-gather.13.cloned.1.call-done = bf16[2048,3,1024]{0,2,1:T(8,128)(2,1)} async-done(((bf16[128,3,1024]{0,2,1:T(8,128)(2,1)}), bf16[2048,3,1024]{0,2,1:T(8,128)(2,1)}) %all-gather.13.cloned.1.call-update) | async-done | bytes 12582928 | tf_op jit(solution)/shard_map/all_gather | solution.py:119
  272.4 60.0 %all-gather.15.cloned.1.call-done = bf16[2048,1024]{1,0:T(8,128)(2,1)} async-done(((bf16[128,1024]{1,0:T(8,128)(2,1)}), bf16[2048,1024]{1,0:T(8,128)(2,1)}) %all-gather.15.cloned.1.call-update) | async-done | bytes 4194320 | tf_op jit(solution)/shard_map/all_gather | solution.py:120
  337.9 31.9 %all-gather.1 = bf16[16,1,128]{2,1,0:T(2,128)(2,1)S(1)} all-gather(bf16[1,1,128]{2,1,0:T(2,128)(2,1)S(1)} %bitcast.179), channel_id=1, replica_groups=mesh['dp'=16,'tensor'=2] {'dp'}, dimensions={0}, use_global_device_ids=true | all-gather | bytes 4352 | tf_op jit(solution)/shard_map/all_gather | solution.py:126
  373.9 226.5 %all-gather.19.cloned.1.call-done = bf16[2048,2,2816]{2,1,0:T(2,128)(2,1)} async-done(((bf16[128,2,2816]{2,1,0:T(2,128)(2,1)}), bf16[2048,2,2816]{2,1,0:T(2,128)(2,1)}) %all-gather.19.cloned.1.call-update) | async-done | bytes 23068688 | tf_op jit(solution)/shard_map/all_gather | solution.py:124
  600.5 24.3 copy.97
  624.7 12.6 fusion.72
  637.3 130.8 %all-gather.21.cloned.1.call-done = bf16[2048,2816]{1,0:T(8,128)(2,1)} async-done(((bf16[128,2816]{1,0:T(8,128)(2,1)}), bf16[2048,2816]{1,0:T(8,128)(2,1)}) %all-gather.21.cloned.1.call-update) | async-done | bytes 11534352 | tf_op jit(solution)/shard_map/all_gather | solution.py:125
  768.1 11.5 multiply_convert_fusion.2
  779.6 12.5 fusion.46
  792.2 10.1 reduce-scatter.13.cloned.1.call-done
  806.5 10.1 all-gather.25.cloned.1.call-done
  822.1 59.6 %while.29 = (s32[]{:T(128)}, f32[8,256,128]{1,2,0:T(8,128)}, f32[8,256,128]{1,2,0:T(8,128)}, bf16[8,256,128]{1,2,0:T(8,128)(2,1)}, bf16[8,256,128]{2,1,0:T(8,128...) while((s32[]{:T(128)}, f32[8,256,128]{1,2,0:T(8,128)}, ...), condition=%wide.region_15.16_spmd.clone, body=%wide.region_13.15_spmd.clone.sunk | while | flops 84770560 | bytes 3026049 | solution.py:192
  884.6 11.5 fusion.61
  896.2 8.4 convolution_convert_fusion.2
  904.7 10.7 convolution_bitcast_fusion.2
  917.1 13.1 fusion.60
  931.3 19.8 fusion.45
  960.7 74.2 %all-reduce.2 = (f32[2048]{0:T(1024)S(1)}, f32[2048]{0:T(1024)S(1)}) all-reduce(f32[2048]{0:T(1024)S(1)} %get-tuple-element.230, f32[2048]{0:T(1024)S(1)} %get-tuple-element.228), channel_id=6, replica_groups=mesh['dp'=16,'tensor'=2] {'dp'}, use_global_device_ids=true, to_apply=%region_19.20.clone | all-reduce | flops 4096 | bytes 32768
  1040.8 358.7 %reduce-scatter.23.cloned.1.call-done = f32[128,2816]{0,1:T(8,128)} async-done(((f32[2048,2816]{0,1:T(8,128)}), f32[128,2816]{0,1:T(8,128)}) %reduce-scatter.23.cloned.1.call-update) | async-done | bytes 1441808 | tf_op jit(solution)/shard_map/reduce_scatter | solution.py:219
  1402.4 367.6 %reduce-scatter.17.cloned.1.call-done = f32[128,3072]{1,0:T(8,128)} async-done(((f32[2048,3072]{1,0:T(8,128)}), f32[128,3072]{1,0:T(8,128)}) %reduce-scatter.17.cloned.1.call-update) | async-done | bytes 1572880 | tf_op jit(solution)/shard_map/reduce_scatter | solution.py:215
  1773.6 937.8 %reduce-scatter.21.cloned.1.call-done = f32[128,5632]{1,0:T(8,128)} async-done(((f32[2048,5632]{1,0:T(8,128)}), f32[128,5632]{1,0:T(8,128)}) %reduce-scatter.21.cloned.1.call-update) | async-done | bytes 2883600 | tf_op jit(solution)/shard_map/reduce_scatter | solution.py:218
  2716.2 180.5 %reduce-scatter.19.cloned.1.call-done = f32[128,1024]{1,0:T(8,128)} async-done(((f32[2048,1024]{1,0:T(8,128)}), f32[128,1024]{1,0:T(8,128)}) %reduce-scatter.19.cloned.1.call-update) | async-done | bytes 524304 | tf_op jit(solution)/shard_map/reduce_scatter | solution.py:216
  (265 shorter events, 140.6 us)
Async XLA Ops:
  7.2 39.0 %copy-start.23 = (s32[1,8]{1,0:T(1,128)S(1)}, s32[1,8]{1,0:T(1,128)}, u32[]{:S(2)}) copy-start(s32[1,8]{1,0:T(1,128)} %param.20) | copy-start | bytes 100
  7.2 49.3 %all-gather.11.cloned.1.call-start = ((), (), s32[]{:S(2)}) async-start(), calls=%async_computation.8 | async-start | bytes 1572864 | tf_op jit(solution)/shard_map/all_gather | solution.py:137
  39.7 221.8 %copy-start.18 = (f32[16,1,128]{2,1,0:T(1,128)}, f32[16,1,128]{2,1,0:T(1,128)S(1)}, u32[]{:S(2)}) copy-start(f32[16,1,128]{2,1,0:T(1,128)S(1)} %convert_element_type.104) | copy-start | bytes 24580
  41.0 220.6 %copy-start.20 = (f32[128]{0:T(128)}, f32[128]{0:T(128)S(1)}, u32[]{:S(2)}) copy-start(f32[128]{0:T(128)S(1)} %add_rsqrt_fusion.1) | copy-start | bytes 1540
  43.0 211.8 %all-gather.13.cloned.1.call-start = ((), (), s32[]{:S(2)}) async-start(), calls=%async_computation.9 | async-start | bytes 13369344 | tf_op jit(solution)/shard_map/all_gather | solution.py:119
  45.4 287.0 %all-gather.15.cloned.1.call-start = ((), (), s32[]{:S(2)}) async-start(), calls=%async_computation.10 | async-start | bytes 4456448 | tf_op jit(solution)/shard_map/all_gather | solution.py:120
  46.1 323.6 %reduce-scatter.9.cloned.1.call-start = ((), (), s32[]{:S(2)}) async-start(), calls=%async_computation.11 | async-start | bytes 3145728 | tf_op jit(solution)/shard_map/reduce_scatter | solution.py:153
  272.3 60.0 %copy-start.15 = (bf16[8,256,128]{2,1,0:T(8,128)(2,1)}, bf16[8,256,128]{2,1,0:T(8,128)(2,1)S(1)}, u32[]{:S(2)}) copy-start(bf16[8,256,128]{2,1,0:T(8,128)(2,1)S(1)} %get-tuple-element.524) | copy-start | bytes 1572868
  272.4 64.8 %copy-start.11 = (bf16[8,256,128]{1,2,0:T(8,128)(2,1)}, bf16[8,256,128]{1,2,0:T(8,128)(2,1)S(1)}, u32[]{:S(2)}) copy-start(bf16[8,256,128]{1,2,0:T(8,128)(2,1)S(1)} %get-tuple-element.100) | copy-start | bytes 1572868
  272.4 64.8 %copy-start.16 = (bf16[8,256,128]{2,1,0:T(8,128)(2,1)}, bf16[8,256,128]{2,1,0:T(8,128)(2,1)S(1)}, u32[]{:S(2)}) copy-start(bf16[8,256,128]{2,1,0:T(8,128)(2,1)S(1)} %get-tuple-element.525) | copy-start | bytes 1572868
  272.4 64.8 %copy-start.17 = (bf16[8,256,128]{2,1,0:T(8,128)(2,1)}, bf16[8,256,128]{2,1,0:T(8,128)(2,1)S(1)}, u32[]{:S(2)}) copy-start(bf16[8,256,128]{2,1,0:T(8,128)(2,1)S(1)} %get-tuple-element.526) | copy-start | bytes 1572868
  337.2 263.2 %all-gather.19.cloned.1.call-start = ((), (), s32[]{:S(2)}) async-start(), calls=%async_computation.13 | async-start | bytes 24510464 | tf_op jit(solution)/shard_map/all_gather | solution.py:124
  337.8 286.9 %all-gather.17.cloned.1.call-start = ((), (), s32[]{:S(2)}) async-start(), calls=%async_computation.12 | async-start | bytes 1572864 | tf_op jit(solution)/shard_map/all_gather | solution.py:160
  372.2 265.1 %all-gather.23.cloned.1.call-start = ((), (), s32[]{:S(2)}) async-start(), calls=%async_computation.16 | async-start | bytes 1572864 | tf_op jit(solution)/shard_map/all_gather | solution.py:174
  373.0 395.1 %all-gather.21.cloned.1.call-start = ((), (), s32[]{:S(2)}) async-start(), calls=%async_computation.14 | async-start | bytes 12255232 | tf_op jit(solution)/shard_map/all_gather | solution.py:125
  373.7 428.6 %reduce-scatter.13.cloned.1.call-start = ((), (), s32[]{:S(2)}) async-start(), calls=%async_computation.17 | async-start | bytes 3145728 | tf_op jit(solution)/shard_map/reduce_scatter | solution.py:181
  792.2 24.4 all-gather.25.cloned.1.call-start
  806.3 152.8 %reduce-scatter.15.cloned.1.call-start = ((), (), s32[]{:S(2)}) async-start(), calls=%async_computation.19 | async-start | bytes 3145728 | tf_op jit(solution)/shard_map/reduce_scatter | solution.py:209
  896.1 141.9 %reduce-scatter.11.cloned.1.call-start = ((), (), s32[]{:S(2)}) async-start(), calls=%async_computation.15 | async-start | bytes 1572864 | tf_op jit(solution)/shard_map/reduce_scatter | solution.py:167
  904.6 494.9 %reduce-scatter.23.cloned.1.call-start = ((), (), s32[]{:S(2)}) async-start(), calls=%async_computation.23 | async-start | bytes 24510464 | tf_op jit(solution)/shard_map/reduce_scatter | solution.py:219
  915.4 854.6 %reduce-scatter.17.cloned.1.call-start = ((), (), s32[]{:S(2)}) async-start(), calls=%async_computation.20 | async-start | bytes 26738688 | tf_op jit(solution)/shard_map/reduce_scatter | solution.py:215
  930.1 1781.3 %reduce-scatter.21.cloned.1.call-start = ((), (), s32[]{:S(2)}) async-start(), calls=%async_computation.22 | async-start | bytes 49020928 | tf_op jit(solution)/shard_map/reduce_scatter | solution.py:218
  951.2 1945.6 %reduce-scatter.19.cloned.1.call-start = ((), (), s32[]{:S(2)}) async-start(), calls=%async_computation.21 | async-start | bytes 8912896 | tf_op jit(solution)/shard_map/reduce_scatter | solution.py:216
  957.2 80.8 %copy-start.2 = (f32[128,2048]{1,0:T(8,128)S(1)}, f32[128,2048]{1,0:T(8,128)}, u32[]{:S(2)}) copy-start(f32[128,2048]{1,0:T(8,128)} %reduce-scatter.13.cloned.1.call-done) | copy-start | bytes 3145732
  (17 other events, 65.5 us)
Sparse Core Ops, SparseCore 0:
  43.1 13.2 all-gather.10
  59.8 194.9 all-gather.12
  257.6 74.7 all-gather.14
  337.3 9.8 reduce-scatter.8
  350.2 250.2 all-gather.18
  602.5 9.3 all-gather.16
  613.6 10.1 all-gather.22
  626.9 141.1 all-gather.20
  792.3 9.9 reduce-scatter.12
  806.4 10.1 all-gather.24
  896.2 10.7 reduce-scatter.14
  909.2 9.6 reduce-scatter.10
  921.3 478.2 reduce-scatter.22
  1405.1 364.8 reduce-scatter.16
  1772.3 939.0 reduce-scatter.20
  2714.1 182.6 reduce-scatter.18

commit v2 on v1

v2 whole, which is shorter than its diff:
```python
import math

import jax
import jax.numpy as jnp
from jax import lax
from jax.sharding import PartitionSpec as P

HEAD_DIM = 128
EPS_NORM = 1e-05
MASKED_SCORE = -1e30
GROUP = 8
THIRDS = (0, 48, 88, 128)
BF = jnp.bfloat16
F32 = jnp.float32


def over_dp(x, bit):
    size = lax.axis_size("dp")
    return lax.ppermute(x, "dp", [(i, i ^ bit) for i in range(size)])


def over_cores(x):
    return lax.ppermute(x, "tensor", [(0, 1), (1, 0)])


def third_cuts(rows):
    return [0, rows * 3 // 8, rows * 11 // 16, rows]


def gather_cube(own):
    cuts = third_cuts(own.shape[0])
    x, y, z = over_dp(own, 1), over_dp(own, 2), over_dp(own, 4)
    xy, yz, zx = over_dp(x, 2), over_dp(y, 4), over_dp(z, 1)
    last = [
        over_dp(xy[: cuts[1]], 4),
        over_dp(yz[cuts[1] : cuts[2]], 1),
        over_dp(zx[cuts[2] :], 2),
    ]
    return [[own], [x], [y], [xy], [z], [zx], [yz], last]


def gather_tokens(own):
    out = []
    for pieces in gather_cube(own):
        out += pieces + [over_cores(piece) for piece in pieces]
    return jnp.concatenate(out, axis=0)


def reduce_tokens(partial):
    cuts = third_cuts(partial.shape[2])
    both = (partial[:, 0].astype(F32) + over_cores(partial[:, 1]).astype(F32)).astype(BF)
    far = both[7]
    parts = [
        over_dp(far[: cuts[1]], 4),
        over_dp(far[cuts[1] : cuts[2]], 1),
        over_dp(far[cuts[2] :], 2),
    ]

    def added(base, index):
        low, high = cuts[index], cuts[index + 1]
        middle = (base[low:high].astype(F32) + parts[index].astype(F32)).astype(BF)
        return jnp.concatenate([base[:low], middle, base[high:]], axis=0)

    xy, yz, zx = added(both[3], 0), added(both[6], 1), added(both[5], 2)

    def plus(base, more):
        return (base.astype(F32) + more.astype(F32)).astype(BF)

    x = plus(both[1], over_dp(xy, 2))
    y = plus(both[2], over_dp(yz, 4))
    z = plus(both[4], over_dp(zx, 1))
    return (
        both[0].astype(F32)
        + over_dp(x, 1).astype(F32)
        + over_dp(y, 2).astype(F32)
        + over_dp(z, 4).astype(F32)
    )


def flip_blocks(x, axis, count, index):
    shape = x.shape
    bit = 1
    while bit < count:
        view = x.reshape(
            shape[:axis] + (count // (2 * bit), 2, bit * (shape[axis] // count)) + shape[axis + 1 :]
        )
        turned = jnp.concatenate(
            [
                lax.slice_in_dim(view, 1, 2, axis=axis + 1),
                lax.slice_in_dim(view, 0, 1, axis=axis + 1),
            ],
            axis=axis + 1,
        )
        x = jnp.where((index & bit) != 0, turned, view).reshape(shape)
        bit *= 2
    return x


def outer_gather(x):
    bit = GROUP
    while bit < lax.axis_size("dp"):
        x = jnp.concatenate([x, over_dp(x, bit)], axis=0)
        bit *= 2
    return x


def outer_reduce(x):
    bit = lax.axis_size("dp") // 2
    while bit >= GROUP:
        half = x.shape[0] // 2
        x = x[:half] + over_dp(x[half:].astype(BF), bit).astype(F32)
        bit //= 2
    return x.astype(BF)


def swap_members(x):
    size = lax.axis_size("dp")
    groups = [list(range(first, first + GROUP)) for first in range(0, size, GROUP)]
    return lax.all_to_all(
        x, "dp", split_axis=0, concat_axis=0, tiled=True, axis_index_groups=groups
    )


def spread_weight(weight):
    rows, which, columns = weight.shape
    own = columns // GROUP
    blocks = jnp.transpose(weight.reshape(rows, which, GROUP, own), (2, 0, 1, 3))
    moved = swap_members(blocks.reshape(GROUP, rows, which * own))
    return outer_gather(moved.reshape(GROUP * rows, which * own))


def return_grad(grad, which):
    summed = outer_reduce(grad)
    rows, own = summed.shape[0] // GROUP, summed.shape[1] // which
    back = swap_members(summed.reshape(GROUP, rows, which * own))
    back = back.reshape(GROUP, rows, which, own).astype(F32)
    return jnp.transpose(back, (1, 2, 0, 3)).reshape(rows, which, GROUP * own)


def doc_layout(lengths, positions):
    docs = jnp.arange(lengths.shape[1], dtype=jnp.int32)
    ends_at = jnp.sum(
        jnp.where(docs[None, None, :] <= docs[None, :, None], lengths[:, None, :], 0),
        axis=2,
        dtype=jnp.int32,
    )
    passed = positions[None, :, None] >= ends_at[:, None, :]
    segment = jnp.sum(passed.astype(jnp.int32), axis=2, dtype=jnp.int32)
    doc_start = jnp.sum(jnp.where(passed, lengths[:, None, :], 0), axis=2, dtype=jnp.int32)
    offset = (positions[None, :] - doc_start).astype(F32)
    allowed = (segment[:, :, None] == segment[:, None, :]) & (
        positions[None, :, None] >= positions[None, None, :]
    )
    half_dim = HEAD_DIM // 2
    inverse = jnp.exp(
        jnp.arange(half_dim, dtype=F32) * (-2.0 * math.log(10000.0) / HEAD_DIM)
    )
    angles = offset[:, :, None] * inverse
    return (allowed, jnp.cos(angles), jnp.sin(angles))


def rotate(values, cosine, sine_part):
    half_dim = HEAD_DIM // 2
    first, second = values[..., :half_dim], values[..., half_dim:]
    return jnp.concatenate(
        [first * cosine - second * sine_part, second * cosine + first * sine_part], axis=-1
    )


def rms_scale(values):
    return lax.rsqrt(jnp.mean(values * values, axis=-1, keepdims=True) + EPS_NORM)


def dot(left, right, contract, batch=((), ())):
    return lax.dot_general(left, right, (contract, batch), preferred_element_type=F32)


NN = ((1,), (0,))
NT = ((1,), (1,))
TN = ((0,), (0,))
ROWS = ((0,), (0,))
B_NN = ((2,), (1,))
B_NT = ((2,), (2,))
B_TN = ((1,), (1,))


def heads_to_tokens(mixed, member):
    rows = mixed.shape[1] // 2
    pair = jnp.concatenate([mixed[:, :rows], over_cores(mixed[:, rows:])], axis=2)
    got = jnp.stack([pair[0]] + [over_dp(pair[k], k) for k in range(1, GROUP)], axis=0)
    got = flip_blocks(got, 0, GROUP, member)
    width = mixed.shape[2]
    return [
        jnp.transpose(part, (1, 0, 2)).reshape(rows, GROUP * width)
        for part in (got[:, :, :width], got[:, :, width:])
    ]


def tokens_to_heads(own, other, member):
    rows, width = own.shape[0], own.shape[1] // GROUP
    halves = [part.reshape(rows, GROUP, width) for part in (own, other)]
    pair = jnp.transpose(jnp.concatenate(halves, axis=2), (1, 0, 2))
    pair = flip_blocks(pair, 0, GROUP, member)
    got = jnp.stack([pair[0]] + [over_dp(pair[k], k) for k in range(1, GROUP)], axis=0)
    return jnp.concatenate([got[:, :, :width], over_cores(got[:, :, width:])], axis=1)


def shards(
    tokens,
    norm1_gain,
    qkv_weight,
    out_weight,
    norm2_gain,
    gate_up_weight,
    down_weight,
    doc_lengths,
    cotangent,
):
    rows, width = tokens.shape
    place = lax.axis_index("dp")
    core = lax.axis_index("tensor")
    member, group = place % GROUP, place // GROUP
    outer = lax.axis_size("dp") // GROUP
    row_count = 2 * rows
    local_width = qkv_weight.shape[2]
    own_width = local_width // GROUP
    heads = own_width // HEAD_DIM
    own_hidden = gate_up_weight.shape[2] // GROUP
    scaling = HEAD_DIM ** (-0.5)

    def rolled(x):
        return flip_blocks(x, 1, outer, group)

    gain_one = norm1_gain.astype(F32)[:, None, None]
    gain_two = norm2_gain.astype(F32)[:, None, None]
    qkv_mat = spread_weight((qkv_weight.astype(F32) * gain_one).astype(BF))
    residual = rolled(tokens).astype(F32)
    scale_one = rms_scale(residual)
    normed_one = residual * scale_one
    rows_one = gather_tokens(normed_one.astype(BF))
    lengths = doc_lengths
    for bit in (1, 2, 4):
        lengths = jnp.concatenate([lengths, over_dp(lengths, bit)], axis=0)
    positions = (jnp.arange(row_count, dtype=jnp.int32) + rows * core) % row_count
    allowed, cosine, sine_part = doc_layout(lengths, positions)
    out_blocks = gather_cube(outer_gather(out_weight))
    out_own = jnp.concatenate([p for block in out_blocks for p in block], axis=0)
    out_other = over_cores(out_own)
    gate_up_mat = spread_weight((gate_up_weight.astype(F32) * gain_two).astype(BF))
    down_mat = spread_weight(down_weight[:, None, :])

    def member_order(x):
        shaped = x.reshape(x.shape[0], outer, GROUP, -1)
        shaped = flip_blocks(shaped, 2, GROUP, member)
        return jnp.swapaxes(shaped, 1, 2).reshape(x.shape)

    def feature_order(x):
        shaped = jnp.swapaxes(x.reshape(x.shape[0], GROUP, outer, -1), 1, 2)
        return flip_blocks(shaped, 2, GROUP, member).reshape(x.shape)

    projected = dot(rows_one, qkv_mat, NN).reshape(GROUP, row_count, 3, heads, HEAD_DIM)
    projected = jnp.moveaxis(projected, 3, 1).reshape(GROUP * heads, row_count, 3, HEAD_DIM)
    if heads > 1:
        allowed, cosine, sine_part = (
            jnp.repeat(part, heads, axis=0) for part in (allowed, cosine, sine_part)
        )
    queries = rotate(projected[:, :, 0], cosine, sine_part).astype(BF)
    keys = rotate(projected[:, :, 1], cosine, sine_part).astype(BF)
    values = projected[:, :, 2].astype(BF)
    scores = dot(queries, keys, B_NT, ROWS) * scaling
    scores = jnp.where(allowed, scores, MASKED_SCORE)
    row_max = jnp.max(scores, axis=2, keepdims=True)
    exp_scores = jnp.exp(scores - row_max)
    row_total = jnp.sum(exp_scores, axis=2, keepdims=True)
    probs = exp_scores / row_total
    weights = probs.astype(BF)
    mixed = dot(weights, values, B_NN, ROWS).astype(BF)
    mixed = jnp.moveaxis(mixed.reshape(GROUP, heads, row_count, HEAD_DIM), 1, 2)
    mixed = mixed.reshape(GROUP, row_count, own_width)
    mixed_own, mixed_other = heads_to_tokens(mixed, member)
    attn = feature_order(dot(mixed_own, out_own, NT) + dot(mixed_other, out_other, NT))
    stream = residual + attn
    scale_two = rms_scale(stream)
    normed_two = stream * scale_two
    rows_two = gather_tokens(normed_two.astype(BF))

    gate_up = dot(rows_two, gate_up_mat, NN)
    gate, upper = gate_up[:, :own_hidden], gate_up[:, own_hidden:]
    sigma = jax.nn.sigmoid(gate)
    silu_gate = gate * sigma
    hidden = (silu_gate * upper).astype(BF)
    cot_own = rolled(cotangent)
    cot_rows = gather_tokens(cot_own)
    grad_hidden = dot(cot_rows, down_mat, NN)
    grad_gate = (grad_hidden * upper * (sigma * (1.0 + gate * (1.0 - sigma)))).astype(BF)
    grad_upper = (grad_hidden * silu_gate).astype(BF)
    grad_gate_up = jnp.concatenate([grad_gate, grad_upper], axis=1)
    part_shape = (GROUP, 2, rows, width)
    back_two = reduce_tokens(dot(grad_gate_up, gate_up_mat, NT).astype(BF).reshape(part_shape))
    down_grad = return_grad(dot(cot_rows, hidden, TN), 1)[:, 0]
    gate_up_plain = return_grad(dot(rows_two, grad_gate_up, TN), 2)
    mlp_out = reduce_tokens(dot(hidden, down_mat, NT).astype(BF).reshape(part_shape))
    output = rolled((stream + mlp_out).astype(BF))

    def norm_back(grad_normed, normed, scale):
        return scale * (
            grad_normed - normed * jnp.mean(grad_normed * normed, axis=-1, keepdims=True)
        )

    grad_stream = cot_own.astype(F32) + norm_back(back_two, normed_two, scale_two)
    grad_low = grad_stream.astype(BF)

    grad_moved = member_order(grad_low)
    mixed_grad = tokens_to_heads(
        dot(grad_moved, out_own, NN).astype(BF), dot(grad_moved, out_other, NN).astype(BF), member
    )
    mixed_grad = jnp.moveaxis(mixed_grad.reshape(GROUP, row_count, heads, HEAD_DIM), 2, 1)
    mixed_grad = mixed_grad.reshape(GROUP * heads, row_count, HEAD_DIM)
    grad_values = dot(weights, mixed_grad, B_TN, ROWS)
    grad_probs = dot(mixed_grad, values, B_NT, ROWS)
    delta_sum = jnp.sum(probs * grad_probs, axis=2, keepdims=True)
    grad_scores = (probs * (grad_probs - delta_sum) * scaling).astype(BF)
    grad_queries = rotate(dot(grad_scores, keys, B_NN, ROWS), cosine, -sine_part)
    grad_keys = rotate(dot(grad_scores, queries, B_TN, ROWS), cosine, -sine_part)
    grad_qkv = jnp.stack([grad_queries, grad_keys, grad_values], axis=2).astype(BF)
    grad_qkv = grad_qkv.reshape(GROUP, heads, row_count, 3, HEAD_DIM)
    grad_qkv = jnp.moveaxis(grad_qkv, 1, 3).reshape(GROUP * row_count, 3 * own_width)
    back_one = reduce_tokens(dot(grad_qkv, qkv_mat, NT).astype(BF).reshape(part_shape))
    qkv_plain = return_grad(dot(rows_one, grad_qkv, TN), 3)
    grad_rows = gather_tokens(grad_low)
    out_grad = return_grad(dot(grad_rows, mixed.reshape(GROUP * row_count, own_width), TN), 1)[:, 0]
    input_grad = rolled((grad_stream + norm_back(back_one, normed_one, scale_one)).astype(BF))

    gains = jnp.stack(
        [
            jnp.sum(qkv_weight.astype(F32) * qkv_plain, axis=(1, 2)),
            jnp.sum(gate_up_weight.astype(F32) * gate_up_plain, axis=(1, 2)),
        ]
    )
    gains = gains + over_cores(gains)
    return (
        output,
        input_grad,
        gains[0],
        qkv_plain * gain_one,
        out_grad,
        gains[1],
        gate_up_plain * gain_two,
        down_grad,
    )


def solution(mesh):
    placed = (
        P(("dp", "tensor"), None),
        P("dp"),
        P("dp", None, "tensor"),
        P("dp", "tensor"),
        P("dp"),
        P("dp", None, "tensor"),
        P("dp", "tensor"),
        P("dp", None),
        P(("dp", "tensor"), None),
    )
    return jax.shard_map(
        shards,
        mesh=mesh,
        in_specs=placed,
        out_specs=(
            P(("dp", "tensor"), None),
            P(("dp", "tensor"), None),
            P("dp"),
            P("dp", None, "tensor"),
            P("dp", "tensor"),
            P("dp"),
            P("dp", None, "tensor"),
            P("dp", "tensor"),
        ),
        check_vma=False,
    )
```

time: 2920 us -> 936 us (0.32)
  waiting for transfers between devices: 2490 us -> 402 us
  local copies, waits for them, and re-layouts: 57.2 us -> 214 us
  blocking collectives: 141 us -> 0 us
  starting transfers between devices: 1.29 us -> 140 us
  matrix products: 177 us -> 105 us
  other arithmetic: 17.9 us -> 58.4 us
    reduce_scatter x8 -> x0, waiting for transfers between devices: 1850 us -> none  [the longest x1 938 us: shards(): lax.psum_scatter(gate_up_part, 'dp', scatter_dimension=0, tiled=True)]
    all_gather x8 -> x0, waiting for transfers between devices: 635 us -> none  [the longest x1 227 us: shards(): lax.all_gather(gate_up_weight, 'dp', axis=0, tiled=True)]
    ppermute x0 -> x144, waiting for transfers between devices: none -> 402 us  [the longest x97 402 us: over_dp(): return lax.ppermute(x, 'dp', [(i, i ^ bit) for i in range(size)])]
    ppermute x0 -> x144, starting transfers between devices: none -> 104 us  [the longest x97 96.4 us: over_dp(): return lax.ppermute(x, 'dp', [(i, i ^ bit) for i in range(size)])]
    dot_general x68 -> x19, matrix products: 177 us -> 101 us  [dot(): lax.dot_general(left, right, (contract, batch), preferred_element_type=F32)]
    unnamed x1 -> x0, blocking collectives: 74.2 us -> none
    all_gather x2 -> x0, blocking collectives: 64.4 us -> none  [the longest x1 32.5 us: shards(): lax.all_gather(norm1_gain, 'dp', axis=0, tiled=True)]
    concatenate x0 -> x8, local copies, waits for them, and re-layouts: none -> 59.8 us  [the longest x4 54.3 us: gather_tokens(): return jnp.concatenate(out, axis=0)]
  transfers between devices with their start and end apart: 16 -> 151, of which waited for: 11 -> 54; matrix products, arithmetic and copies ran while one was open for 5% -> 33% of each run, Pallas kernels for 0% -> 0%
where the time goes in v2:
time: 936 us; the launch traced here: 923 us
  waiting for transfers between devices  402 us (43%)
  local copies, waits for them, and re-layouts  214 us (23%)
  starting transfers between devices  140 us (15%)
  matrix products  105 us (11%)
  other arithmetic  58.4 us (6%)
    ppermute x97, waiting for transfers between devices, over_dp(): return lax.ppermute(x, 'dp', [(i, i ^ bit) for i in range(size)])  402 us
    dot_general x19, matrix products, dot(): lax.dot_general(left, right, (contract, batch), preferred_element_type=F32)  101 us
    ppermute x97, starting transfers between devices, over_dp(): return lax.ppermute(x, 'dp', [(i, i ^ bit) for i in range(size)])  96.4 us
    unnamed x253, local copies, waits for them, and re-layouts  93.7 us
    concatenate x4, local copies, waits for them, and re-layouts, gather_tokens(): return jnp.concatenate(out, axis=0)  54.3 us
    all_to_all x7, starting transfers between devices, swap_members(): lax.all_to_all(x, 'dp', split_axis=0, concat_axis=0, tiled=True, axis_ind...  36.4 us
  transfers between devices with their start and end apart: 151, of which 54 were waited for; matrix products, arithmetic and copies ran while one was open for 33% of the time, Pallas kernels for 0%

profile of v2, /device:TPU:24, one launch (start us, length us, event | category | flops | bytes accessed | tf_op | source)
XLA Modules:
  0.0 922.9 jit_solution(13654986081889914157)
XLA Ops:
  8.3 9.6 %collective-permute-done = s32[1,8]{1,0:T(1,128)S(1)} collective-permute-done((s32[1,8]{1,0:T(1,128)S(1)}, s32[1,8]{1,0:T(1,128)S(1)}, u32[]{:S(2)}, u32[]{:S(2)}) %collective-permute-start) | collective-permute-done | bytes 64 | tf_op jit(solution)/shard_map/ppermute | solution.py:19
  62.2 7.8 collective-permute-done.12
  93.6 13.3 %collective-permute-done.18 = bf16[40,2048]{0,1:T(8,128)(2,1)} collective-permute-done((bf16[40,2048]{0,1:T(8,128)(2,1)}, bf16[40,2048]{0,1:T(8,128)(2,1)}, u32[]{:S(2)}, u32[]{:S(2)}) %collective-permute-start.18) | collective-permute-done | bytes 163872 | tf_op jit(solution)/shard_map/ppermute | solution.py:19
  111.7 10.7 %collective-permute-done.16 = bf16[48,2048]{0,1:T(8,128)(2,1)S(1)} collective-permute-done((bf16[48,2048]{0,1:T(8,128)(2,1)}, bf16[48,2048]{0,1:T(8,128)(2,1)S(1)}, u32[]{:S(2)}, u32[]{:S(2)}) %collective-permute-start.16) | collective-permute-done | bytes 196640 | tf_op jit(solution)/shard_map/ppermute | solution.py:19
  143.9 13.5 %concatenate.239 = bf16[2048,2048]{0,1:T(8,128)(2,1)} concatenate(bf16[128,2048]{0,1:T(8,128)(2,1)S(1)} %copy-done.29, bf16[128,2048]{0,1:T(8,128)(2,1)} %collective-permute-done.3, bf16[128,2048]{0,1:T(8,128)(2,1)} %collective-permute-done.4, bf16[128,2048]{0,1:T(8,128)(2,1)} %copy-done.55, bf16[128,2048]{0,1:T(8,128)(2,1)} %collective-permute-done.6, ...), dimensions={0} | concatenate | bytes 16777216 | tf_op jit(solution)/shard_map/concatenate | solution.py:46
  196.9 15.7 %collective-permute-done.25 = bf16[128,256]{1,0:T(8,128)(2,1)S(1)} collective-permute-done((bf16[128,256]{1,0:T(8,128)(2,1)S(1)}, bf16[128,256]{1,0:T(8,128)(2,1)S(1)}, u32[]{:S(2)}, u32[]{:S(2)}) %collective-permute-start.25) | collective-permute-done | bytes 65568 | tf_op jit(solution)/shard_map/ppermute | solution.py:19
  272.5 9.1 collective-permute-done.88
  290.0 90.4 %collective-permute-done.62 = bf16[1024,352]{0,1:T(8,128)(2,1)S(1)} collective-permute-done((bf16[1024,352]{0,1:T(8,128)(2,1)S(1)}, bf16[1024,352]{0,1:T(8,128)(2,1)S(1)}, u32[]{:S(2)}, u32[]{:S(2)}) %collective-permute-start.62) | collective-permute-done | bytes 720928 | tf_op jit(solution)/shard_map/ppermute | solution.py:19
  382.4 12.3 %collective-permute-done.51 = bf16[128,2048]{0,1:T(8,128)(2,1)S(1)} collective-permute-done((bf16[128,2048]{0,1:T(8,128)(2,1)S(1)}, bf16[128,2048]{0,1:T(8,128)(2,1)S(1)}, u32[]{:S(2)}, u32[]{:S(2)}) %collective-permute-start.51) | collective-permute-done | bytes 524320 | tf_op jit(solution)/shard_map/ppermute | solution.py:19
  398.9 10.6 %collective-permute-done.57 = bf16[40,2048]{0,1:T(8,128)(2,1)} collective-permute-done((bf16[40,2048]{0,1:T(8,128)(2,1)S(1)}, bf16[40,2048]{0,1:T(8,128)(2,1)}, u32[]{:S(2)}, u32[]{:S(2)}) %collective-permute-start.57) | collective-permute-done | bytes 163872 | tf_op jit(solution)/shard_map/ppermute | solution.py:19
  411.6 13.5 %concatenate.276 = bf16[2048,2048]{0,1:T(8,128)(2,1)} concatenate(bf16[128,2048]{0,1:T(8,128)(2,1)} %bitcast_select_fusion.3, bf16[128,2048]{0,1:T(8,128)(2,1)} %collective-permute-done.73, bf16[128,2048]{0,1:T(8,128)(2,1)} %collective-permute-done.74, bf16[128,2048]{0,1:T(8,128)(2,1)} %collective-permute-done.75, bf16[128,2048]{0,1:T(8,128)(2,1)} %collective-permute-done.76, ...), dimensions={0} | concatenate | bytes 16777216 | tf_op jit(solution)/shard_map/concatenate | solution.py:46
  432.4 13.6 %concatenate.266 = bf16[2048,2048]{0,1:T(8,128)(2,1)} concatenate(bf16[128,2048]{0,1:T(8,128)(2,1)S(1)} %copy-done.21, bf16[128,2048]{0,1:T(8,128)(2,1)} %copy-done.63, bf16[128,2048]{0,1:T(8,128)(2,1)} %collective-permute-done.43, bf16[128,2048]{0,1:T(8,128)(2,1)} %collective-permute-done.44, bf16[128,2048]{0,1:T(8,128)(2,1)} %collective-permute-done.45, ...), dimensions={0} | concatenate | bytes 16777216 | tf_op jit(solution)/shard_map/concatenate | solution.py:46
  445.9 9.7 %fusion.170 = f32[2048,704]{0,1:T(8,128)S(1)} fusion(bf16[2048,704]{0,1:T(8,128)(2,1)} %copy-done.45, bf16[2048,2048]{0,1:T(8,128)(2,1)} %concatenate.266), kind=kOutput, calls=%fused_computation.406 | convolution fusion | flops 5905580032 | bytes 17039360 | tf_op jit(solution)/shard_map/dot_general | solution.py:175
  455.6 8.8 multiply_convert_fusion.1
  511.9 11.0 %fusion.12 = f32[2048,704]{0,1:T(8,128)} fusion(bf16[2048,2048]{0,1:T(8,128)(2,1)} %concatenate.266, bf16[2048,352]{0,1:T(8,128)(2,1)} %copy-done.99, bf16[2048,352]{0,1:T(8,128)(2,1)S(1)} %copy-done.98), kind=kOutput, calls=%fused_computation.34 | convolution fusion | flops 5911347200 | bytes 17039360 | tf_op jit(solution)/shard_map/dot_general | solution.py:175
  535.7 10.0 %collective-permute-done.96 = bf16[40,2048]{0,1:T(8,128)(2,1)S(1)} collective-permute-done((bf16[40,2048]{0,1:T(8,128)(2,1)}, bf16[40,2048]{0,1:T(8,128)(2,1)S(1)}, u32[]{:S(2)}, u32[]{:S(2)}) %collective-permute-start.96) | collective-permute-done | bytes 163872 | tf_op jit(solution)/shard_map/ppermute | solution.py:19
  548.5 8.4 collective-permute-done.67
  619.4 44.9 %collective-permute-done.143 = bf16[1024,352]{0,1:T(8,128)(2,1)S(1)} collective-permute-done((bf16[1024,352]{0,1:T(8,128)(2,1)S(1)}, bf16[1024,352]{0,1:T(8,128)(2,1)S(1)}, u32[]{:S(2)}, u32[]{:S(2)}) %collective-permute-start.143) | collective-permute-done | bytes 720928 | tf_op jit(solution)/shard_map/ppermute | solution.py:19
  686.3 19.3 %collective-permute-done.105 = bf16[128,256]{1,0:T(8,128)(2,1)S(1)} collective-permute-done((bf16[128,256]{1,0:T(8,128)(2,1)S(1)}, bf16[128,256]{1,0:T(8,128)(2,1)S(1)}, u32[]{:S(2)}, u32[]{:S(2)}) %collective-permute-start.105) | collective-permute-done | bytes 65568 | tf_op jit(solution)/shard_map/ppermute | solution.py:19
  784.9 9.3 %collective-permute-done.138 = bf16[40,2048]{0,1:T(8,128)(2,1)} collective-permute-done((bf16[40,2048]{0,1:T(8,128)(2,1)}, bf16[40,2048]{0,1:T(8,128)(2,1)}, u32[]{:S(2)}, u32[]{:S(2)}) %collective-permute-start.138) | collective-permute-done | bytes 163872 | tf_op jit(solution)/shard_map/ppermute | solution.py:19
  798.0 7.4 fusion.167
  815.6 13.7 %concatenate.310 = bf16[2048,2048]{0,1:T(8,128)(2,1)} concatenate(bf16[128,2048]{0,1:T(8,128)(2,1)S(1)} %get-tuple-element.34, bf16[128,2048]{0,1:T(8,128)(2,1)} %collective-permute-done.123, bf16[128,2048]{0,1:T(8,128)(2,1)} %collective-permute-done.124, bf16[128,2048]{0,1:T(8,128)(2,1)} %collective-permute-done.125, bf16[128,2048]{0,1:T(8,128)(2,1)} %collective-permute-done.126, ...), dimensions={0} | concatenate | bytes 16777216 | tf_op jit(solution)/shard_map/concatenate | solution.py:46
  837.5 12.9 %collective-permute-done.120 = bf16[1024,384]{1,0:T(8,128)(2,1)S(1)} collective-permute-done((bf16[1024,384]{1,0:T(8,128)(2,1)S(1)}, bf16[1024,384]{1,0:T(8,128)(2,1)S(1)}, u32[]{:S(2)}, u32[]{:S(2)}) %collective-permute-start.120) | collective-permute-done | bytes 786464 | tf_op jit(solution)/shard_map/ppermute | solution.py:19
  866.4 11.8 %collective-permute-done.114 = bf16[40,2048]{0,1:T(8,128)(2,1)S(1)} collective-permute-done((bf16[40,2048]{0,1:T(8,128)(2,1)S(1)}, bf16[40,2048]{0,1:T(8,128)(2,1)S(1)}, u32[]{:S(2)}, u32[]{:S(2)}) %collective-permute-start.114) | collective-permute-done | bytes 163872 | tf_op jit(solution)/shard_map/ppermute | solution.py:19
  (731 shorter events, 532.6 us)
Async XLA Ops:
  29.3 58.0 %all-to-all-start = ((bf16[8,128,384]{1,2,0:T(8,128)(2,1)}), bf16[8,128,384]{1,2,0:T(8,128)(2,1)S(1)}, u32[]{:S(2)}, u32[]{:S(2)}) async-start(bf16[8,128,384]{1,2,0:T(8,128)(2,1)} %bitcast.3), calls=%async_computation | async-start | bytes 1572864 | tf_op jit(solution)/shard_map/all_to_all | solution.py:119
  75.2 49.2 %collective-permute-start.36 = (bf16[256,1024]{1,0:T(8,128)(2,1)}, bf16[256,1024]{1,0:T(8,128)(2,1)}, u32[]{:S(2)}, u32[]{:S(2)}) collective-permute-start(bf16[256,1024]{1,0:T(8,128)(2,1)} %collective-permute-done.35), channel_id=1, source_target_pairs={{0,2},{2,0},{4,6},{6,4},{8,10},{10,8},{12,14},{14,12},{16,18},{18,... | collective-permute-start | bytes 1572872 | tf_op jit(solution)/shard_map/ppermute | solution.py:19
  75.9 48.8 %collective-permute-start.37 = (bf16[256,1024]{1,0:T(8,128)(2,1)}, bf16[256,1024]{1,0:T(8,128)(2,1)}, u32[]{:S(2)}, u32[]{:S(2)}) collective-permute-start(bf16[256,1024]{1,0:T(8,128)(2,1)} %collective-permute-done.33), channel_id=1, source_target_pairs={{0,8},{2,10},{4,12},{6,14},{8,0},{10,2},{12,4},{14,6},{16,24},{18,... | collective-permute-start | bytes 1572872 | tf_op jit(solution)/shard_map/ppermute | solution.py:19
  77.2 47.7 %collective-permute-start.34 = (bf16[256,1024]{1,0:T(8,128)(2,1)}, bf16[256,1024]{1,0:T(8,128)(2,1)S(1)}, u32[]{:S(2)}, u32[]{:S(2)}) collective-permute-start(bf16[256,1024]{1,0:T(8,128)(2,1)} %collective-permute-done.32), channel_id=1, source_target_pairs={{0,4},{2,6},{4,0},{6,2},{8,12},{10,14},{12,8},{14,10},{16,20},{18,... | collective-permute-start | bytes 1572872 | tf_op jit(solution)/shard_map/ppermute | solution.py:19
  87.3 100.1 %all-to-all-start.2 = ((bf16[8,128,352]{1,2,0:T(8,128)(2,1)}), bf16[8,128,352]{1,2,0:T(8,128)(2,1)}, u32[]{:S(2)}, u32[]{:S(2)}) async-start(bf16[8,128,352]{1,2,0:T(8,128)(2,1)} %bitcast.514), calls=%async_computation.2 | async-start | bytes 1441792 | tf_op jit(solution)/shard_map/all_to_all | solution.py:119
  111.3 46.1 %collective-permute-start.22 = (bf16[1024,384]{1,0:T(8,128)(2,1)}, bf16[1024,384]{1,0:T(8,128)(2,1)}, u32[]{:S(2)}, u32[]{:S(2)}) collective-permute-start(bf16[1024,384]{1,0:T(8,128)(2,1)} %bitcast.531), channel_id=1, source_target_pairs={{0,16},{2,18},{4,20},{6,22},{8,24},{10,26},{12,28},{14,30},{16,0},... | collective-permute-start | bytes 2359304 | tf_op jit(solution)/shard_map/ppermute | solution.py:19
  140.1 94.6 %collective-permute-start.74 = (bf16[128,2048]{0,1:T(8,128)(2,1)}, bf16[128,2048]{0,1:T(8,128)(2,1)}, u32[]{:S(2)}, u32[]{:S(2)}) collective-permute-start(bf16[128,2048]{0,1:T(8,128)(2,1)} %bitcast_select_fusion.3), channel_id=1, source_target_pairs={{0,2},{2,0},{4,6},{6,4},{8,10},{10,8},{12,14},{14,12},{16,18},{18,... | collective-permute-start | bytes 1572872 | tf_op jit(solution)/shard_map/ppermute | solution.py:19
  141.5 125.4 %collective-permute-start.73 = (bf16[128,2048]{0,1:T(8,128)(2,1)}, bf16[128,2048]{0,1:T(8,128)(2,1)}, u32[]{:S(2)}, u32[]{:S(2)}) collective-permute-start(bf16[128,2048]{0,1:T(8,128)(2,1)} %bitcast_select_fusion.3), channel_id=1, source_target_pairs={{0,1},{1,0},{2,3},{3,2},{4,5},{5,4},{6,7},{7,6},{8,9},{9,8},{10,11... | collective-permute-start | bytes 1572872 | tf_op jit(solution)/shard_map/ppermute | solution.py:23
  182.3 86.5 %collective-permute-start.81 = (bf16[128,2048]{0,1:T(8,128)(2,1)}, bf16[128,2048]{0,1:T(8,128)(2,1)}, u32[]{:S(2)}, u32[]{:S(2)}) collective-permute-start(bf16[128,2048]{0,1:T(8,128)(2,1)} %collective-permute-done.80), channel_id=1, source_target_pairs={{0,1},{1,0},{2,3},{3,2},{4,5},{5,4},{6,7},{7,6},{8,9},{9,8},{10,11... | collective-permute-start | bytes 1572872 | tf_op jit(solution)/shard_map/ppermute | solution.py:23
  185.9 56.2 %collective-permute-start.41 = (bf16[2048,1024]{1,0:T(8,128)(2,1)}, bf16[2048,1024]{1,0:T(8,128)(2,1)}, u32[]{:S(2)}, u32[]{:S(2)}) collective-permute-start(bf16[2048,1024]{1,0:T(8,128)(2,1)} %constant_dynamic-update-slice_fusion.10), channel_id=1, source_target_pairs={{0,1},{1,0},{2,3},{3,2},{4,5},{5,4},{6,7},{7,6},{8,9},{9,8},{10,11... | collective-permute-start | bytes 12582920 | tf_op jit(solution)/shard_map/ppermute | solution.py:23
  187.4 53.4 %all-to-all-start.1 = ((bf16[8,128,704]{1,2,0:T(8,128)(2,1)}), bf16[8,128,704]{1,2,0:T(8,128)(2,1)S(1)}, u32[]{:S(2)}, u32[]{:S(2)}) async-start(bf16[8,128,704]{1,2,0:T(8,128)(2,1)} %bitcast.489), calls=%async_computation.1 | async-start | bytes 2883584 | tf_op jit(solution)/shard_map/all_to_all | solution.py:119
  283.9 97.7 %collective-permute-start.61 = (bf16[1024,704]{0,1:T(8,128)(2,1)S(1)}, bf16[1024,704]{0,1:T(8,128)(2,1)S(1)}, u32[]{:S(2)}, u32[]{:S(2)}) collective-permute-start(bf16[1024,704]{0,1:T(8,128)(2,1)S(1)} %copy-done.39), channel_id=1, source_target_pairs={{0,16},{2,18},{4,20},{6,22},{8,24},{10,26},{12,28},{14,30},{16,0},... | collective-permute-start | bytes 4325384 | tf_op jit(solution)/shard_map/ppermute | solution.py:19
  286.6 93.7 %collective-permute-start.62 = (bf16[1024,352]{0,1:T(8,128)(2,1)S(1)}, bf16[1024,352]{0,1:T(8,128)(2,1)S(1)}, u32[]{:S(2)}, u32[]{:S(2)}) collective-permute-start(bf16[1024,352]{0,1:T(8,128)(2,1)S(1)} %copy-done.47), channel_id=1, source_target_pairs={{0,16},{2,18},{4,20},{6,22},{8,24},{10,26},{12,28},{14,30},{16,0},... | collective-permute-start | bytes 2162696 | tf_op jit(solution)/shard_map/ppermute | solution.py:19
  287.9 92.5 %collective-permute-start.49 = (bf16[128,2048]{0,1:T(8,128)(2,1)S(1)}, bf16[128,2048]{0,1:T(8,128)(2,1)S(1)}, u32[]{:S(2)}, u32[]{:S(2)}) collective-permute-start(bf16[128,2048]{0,1:T(8,128)(2,1)S(1)} %multiply_convert_fusion.4), channel_id=1, source_target_pairs={{0,8},{2,10},{4,12},{6,14},{8,0},{10,2},{12,4},{14,6},{16,24},{18,... | collective-permute-start | bytes 1572872 | tf_op jit(solution)/shard_map/ppermute | solution.py:19
  288.3 93.3 %collective-permute-start.45 = (bf16[128,2048]{0,1:T(8,128)(2,1)S(1)}, bf16[128,2048]{0,1:T(8,128)(2,1)}, u32[]{:S(2)}, u32[]{:S(2)}) collective-permute-start(bf16[128,2048]{0,1:T(8,128)(2,1)S(1)} %multiply_convert_fusion.4), channel_id=1, source_target_pairs={{0,4},{2,6},{4,0},{6,2},{8,12},{10,14},{12,8},{14,10},{16,20},{18,... | collective-permute-start | bytes 1572872 | tf_op jit(solution)/shard_map/ppermute | solution.py:19
  289.3 92.5 %collective-permute-start.43 = (bf16[128,2048]{0,1:T(8,128)(2,1)S(1)}, bf16[128,2048]{0,1:T(8,128)(2,1)}, u32[]{:S(2)}, u32[]{:S(2)}) collective-permute-start(bf16[128,2048]{0,1:T(8,128)(2,1)S(1)} %multiply_convert_fusion.4), channel_id=1, source_target_pairs={{0,2},{2,0},{4,6},{6,4},{8,10},{10,8},{12,14},{14,12},{16,18},{18,... | collective-permute-start | bytes 1572872 | tf_op jit(solution)/shard_map/ppermute | solution.py:19
  600.2 64.2 %collective-permute-start.143 = (bf16[1024,352]{0,1:T(8,128)(2,1)S(1)}, bf16[1024,352]{0,1:T(8,128)(2,1)S(1)}, u32[]{:S(2)}, u32[]{:S(2)}) collective-permute-start(bf16[1024,352]{0,1:T(8,128)(2,1)S(1)} %slice.1064), channel_id=1, source_target_pairs={{0,16},{2,18},{4,20},{6,22},{8,24},{10,26},{12,28},{14,30},{16,0},... | collective-permute-start | bytes 2162696 | tf_op jit(solution)/shard_map/ppermute | solution.py:19
  601.7 104.2 %collective-permute-start.121 = (bf16[1024,704]{0,1:T(8,128)(2,1)}, bf16[1024,704]{0,1:T(8,128)(2,1)}, u32[]{:S(2)}, u32[]{:S(2)}) collective-permute-start(bf16[1024,704]{0,1:T(8,128)(2,1)} %slice.1062), channel_id=1, source_target_pairs={{0,16},{2,18},{4,20},{6,22},{8,24},{10,26},{12,28},{14,30},{16,0},... | collective-permute-start | bytes 4325384 | tf_op jit(solution)/shard_map/ppermute | solution.py:19
  618.2 55.5 %collective-permute-start.102 = (bf16[128,256]{1,0:T(8,128)(2,1)S(1)}, bf16[128,256]{1,0:T(8,128)(2,1)S(1)}, u32[]{:S(2)}, u32[]{:S(2)}) collective-permute-start(bf16[128,256]{1,0:T(8,128)(2,1)S(1)} %get-tuple-element.112), channel_id=1, source_target_pairs={{0,2},{2,0},{4,6},{6,4},{8,10},{10,8},{12,14},{14,12},{16,18},{18,... | collective-permute-start | bytes 196616 | tf_op jit(solution)/shard_map/ppermute | solution.py:19
  665.4 59.4 %all-to-all-start.6 = ((bf16[8,128,352]{1,2,0:T(8,128)(2,1)}), bf16[8,128,352]{1,2,0:T(8,128)(2,1)S(1)}, u32[]{:S(2)}, u32[]{:S(2)}) async-start(bf16[8,128,352]{1,2,0:T(8,128)(2,1)} %copy_bitcast_fusion.3), calls=%async_computation.6 | async-start | bytes 1441792 | tf_op jit(solution)/shard_map/all_to_all | solution.py:119
  710.8 53.4 %collective-permute-start.124 = (bf16[128,2048]{0,1:T(8,128)(2,1)S(1)}, bf16[128,2048]{0,1:T(8,128)(2,1)}, u32[]{:S(2)}, u32[]{:S(2)}) collective-permute-start(bf16[128,2048]{0,1:T(8,128)(2,1)S(1)} %get-tuple-element.34), channel_id=1, source_target_pairs={{0,2},{2,0},{4,6},{6,4},{8,10},{10,8},{12,14},{14,12},{16,18},{18,... | collective-permute-start | bytes 1572872 | tf_op jit(solution)/shard_map/ppermute | solution.py:19
  725.7 44.1 %all-to-all-start.4 = ((bf16[8,128,704]{1,2,0:T(8,128)(2,1)}), bf16[8,128,704]{1,2,0:T(8,128)(2,1)S(1)}, u32[]{:S(2)}, u32[]{:S(2)}) async-start(bf16[8,128,704]{1,2,0:T(8,128)(2,1)} %copy_bitcast_fusion.1), calls=%async_computation.4 | async-start | bytes 2883584 | tf_op jit(solution)/shard_map/all_to_all | solution.py:119
  763.7 93.7 %collective-permute-start.110 = (bf16[8,128,2048]{1,2,0:T(8,128)(2,1)}, bf16[8,128,2048]{1,2,0:T(8,128)(2,1)}, u32[]{:S(2)}, u32[]{:S(2)}) collective-permute-start(bf16[8,128,2048]{1,2,0:T(8,128)(2,1)} %bitcast.507), channel_id=1, source_target_pairs={{0,1},{1,0},{2,3},{3,2},{4,5},{5,4},{6,7},{7,6},{8,9},{9,8},{10,11... | collective-permute-start | bytes 12582920 | tf_op jit(solution)/shard_map/ppermute | solution.py:23
  807.1 43.3 %collective-permute-start.120 = (bf16[1024,384]{1,0:T(8,128)(2,1)S(1)}, bf16[1024,384]{1,0:T(8,128)(2,1)S(1)}, u32[]{:S(2)}, u32[]{:S(2)}) collective-permute-start(bf16[1024,384]{1,0:T(8,128)(2,1)S(1)} %slice.1063), channel_id=1, source_target_pairs={{0,16},{2,18},{4,20},{6,22},{8,24},{10,26},{12,28},{14,30},{16,0},... | collective-permute-start | bytes 2359304 | tf_op jit(solution)/shard_map/ppermute | solution.py:19
  (232 other events, 4388.3 us)

commit v3 on v2

v3 whole, which is shorter than its diff:
```python
import functools
import math

import jax
import jax.numpy as jnp
from jax import lax
from jax.experimental import pallas as pl
from jax.experimental.pallas import tpu as pltpu
from jax.sharding import PartitionSpec as P

HEAD_DIM = 128
EPS_NORM = 1e-05
MASKED_SCORE = -1e30
GROUP = 8
X, Y, Z = 1, 2, 8
NEXT = 4
ORDER = (0, 1, 2, 4, 3, 6, 5, 7)
BF = jnp.bfloat16
F32 = jnp.float32
VMEM_LIMIT = 60 * 2**20


def over_dp(x, bit):
    size = lax.axis_size("dp")
    return lax.ppermute(x, "dp", [(i, i ^ bit) for i in range(size)])


def over_cores(x):
    return lax.ppermute(x, "tensor", [(0, 1), (1, 0)])


def outer_bits():
    size = lax.axis_size("dp")
    return [NEXT] + [1 << i for i in range(4, 12) if 1 << i < size]


def groups():
    size = lax.axis_size("dp")
    members = [x + y + z for z in (0, Z) for y in (0, Y) for x in (0, X)]
    firsts = [i for i in range(size) if not i & (X | Y | Z)]
    return [[first + member for member in members] for first in firsts]


def flip_blocks(x, axis, count, index):
    shape = x.shape
    bit = 1
    while bit < count:
        view = x.reshape(
            shape[:axis] + (count // (2 * bit), 2, bit * (shape[axis] // count)) + shape[axis + 1 :]
        )
        turned = jnp.concatenate(
            [
                lax.slice_in_dim(view, 1, 2, axis=axis + 1),
                lax.slice_in_dim(view, 0, 1, axis=axis + 1),
            ],
            axis=axis + 1,
        )
        x = jnp.where((index & bit) != 0, turned, view).reshape(shape)
        bit *= 2
    return x


def after(x, *others):
    return lax.optimization_barrier((x, *others))[0]


def after_all(arrays, *others):
    return list(lax.optimization_barrier((*arrays, *others)))[: len(arrays)]


def with_other_core(blocks):
    return [array for block in blocks for array in (block, over_cores(block))]


def part_of(pieces, first, rows):
    moves = [(i, first, i // 2, (i % 2) * rows, rows) for i in range(len(pieces))]
    return pieces, tuple(moves)


def gather(own):
    x, y, z = over_dp(own, X), over_dp(own, Y), over_dp(own, Z)
    xy, zx, yz = over_dp(x, Y), over_dp(z, X), over_dp(z, Y)
    far = over_dp(yz, X)
    return [own, x, y, z, xy, yz, zx, far]


def plus(base, more):
    return (base.astype(F32) + more.astype(F32)).astype(BF)


def both_cores(own, other):
    other = over_cores(other)
    return [plus(own[step], other[step]) for step in range(GROUP)]


def reduce_first(blocks):
    own, x, y, z, xy, yz, zx, far = blocks
    return [own, plus(x, over_dp(xy, Y)), y, plus(z, over_dp(zx, X)), plus(yz, over_dp(far, X))]


def reduce_second(blocks):
    own, x, y, z, yz = blocks
    return [own, x, y, plus(z, over_dp(yz, Y))]


def reduce_last(own, x, y, z):
    terms = [own, over_dp(x, X), over_dp(y, Y), over_dp(z, Z)]
    return sum(term.astype(F32) for term in terms)


def swap_members(blocks):
    return lax.all_to_all(
        blocks, "dp", split_axis=0, concat_axis=0, tiled=True, axis_index_groups=groups()
    )


def outer_gather(block):
    blocks = [block]
    for bit in outer_bits():
        blocks += [over_dp(one, bit) for one in blocks]
    return blocks


def outer_reduce(part):
    size = lax.axis_size("dp")
    across = [[i for i in range(size) if i & (X | Y | Z) == low] for low in range(size) if not low & ~(X | Y | Z)]
    outer = len(across[0])
    got = lax.all_to_all(
        part.reshape(outer, GROUP, *part.shape[1:]),
        "dp",
        split_axis=0,
        concat_axis=0,
        tiled=True,
        axis_index_groups=across,
    )
    return jnp.sum(got.astype(F32), axis=0).astype(BF)


def dot(left, right, left_dim, right_dim):
    return lax.dot_general(
        left, right, (((left_dim,), (right_dim,)), ((), ())), preferred_element_type=F32
    )


def moves_of(moves, piece_refs, held, sems):
    return [
        (
            step,
            pltpu.make_async_copy(
                piece_refs[index].at[pl.ds(source, rows)],
                held.at[step, pl.ds(row, rows)],
                sems.at[index],
            ),
        )
        for index, source, step, row, rows in moves
    ]


def fetch(moves, piece_refs, held, sems, step):
    copies = moves_of(moves, piece_refs, held, sems)

    @pl.when(step == 0)
    def _():
        for _, copy in copies:
            copy.start()

    for index in range(GROUP):

        @pl.when(step == index)
        def _():
            for at, copy in copies:
                if at == index:
                    copy.wait()


def turned(values, cosine, sine):
    return values * cosine + pltpu.roll(values, HEAD_DIM // 2, 1) * sine


def probabilities(queries, keys, mask):
    scores = dot(queries, keys, 1, 1) * (HEAD_DIM**-0.5)
    scores = jnp.where(mask > 0, scores, MASKED_SCORE)
    exps = jnp.exp(scores - jnp.max(scores, axis=1, keepdims=True))
    return exps / jnp.sum(exps, axis=1, keepdims=True)


def params():
    return pltpu.CompilerParams(
        dimension_semantics=("arbitrary",), vmem_limit_bytes=VMEM_LIMIT
    )


def whole(array):
    return pl.BlockSpec(array.shape, lambda step, places: (0,) * array.ndim)


def stepped(*block):
    return pl.BlockSpec((1, *block), lambda step, places: (step,) + (0,) * len(block))


ANYWHERE = pl.BlockSpec(memory_space=pl.ANY)


def fetch_weights(refs, held, sems, step):
    blocks = refs[0].shape[0]
    copies = [
        pltpu.make_async_copy(ref, held.at[pl.ds(i * blocks, blocks)], sems.at[i])
        for i, ref in enumerate(refs)
    ]

    @pl.when(step == 0)
    def _():
        for copy in copies:
            copy.start()

    def wait():
        @pl.when(step == 0)
        def _():
            for copy in copies:
                copy.wait()

    return wait


def head_weights(held, rows):
    owners = held.shape[0]
    cut = 3 * HEAD_DIM
    return (
        held[:, :rows, :cut].reshape(owners * rows, cut),
        held[:, :rows, cut:].reshape(owners * rows, HEAD_DIM),
    )


def attend_kernel(moves, shard_rows, outer, places, cosine, sine, mask, *refs):
    weights, refs = refs[:outer], refs[outer:]
    count = len(moves)
    pieces, refs = refs[:count], refs[count:]
    a_own, a_other, mixed_ref, q_ref, k_ref, v_ref, held, weight, sems, weight_sems = refs
    step = pl.program_id(0)
    wait = fetch_weights(weights, weight, weight_sems, step)
    fetch(moves, pieces, held, sems, step)
    wait()
    qkv_w, out_w = head_weights(weight, shard_rows)
    projected = dot(held[step], qkv_w, 1, 0)
    width = HEAD_DIM
    queries = turned(projected[:, :width], cosine[0], sine[0]).astype(BF)
    keys = turned(projected[:, width : 2 * width], cosine[0], sine[0]).astype(BF)
    values = projected[:, 2 * width :].astype(BF)
    q_ref[0], k_ref[0], v_ref[0] = queries, keys, values
    probs = probabilities(queries, keys, mask[0]).astype(BF)
    mixed = dot(probs, values, 1, 0).astype(BF)
    mixed_ref[0] = mixed
    attn = dot(mixed, out_w, 1, 1).astype(BF)
    half = attn.shape[0] // 2
    a_own[0], a_other[0] = attn[:half], attn[half:]


def row_specs(tokens):
    return [stepped(tokens, HEAD_DIM), stepped(tokens, HEAD_DIM), stepped(tokens, tokens)]


def attend(places, rows_one, weights, shard_rows, cosine, sine, mask):
    arrays, moves = rows_one
    tokens, width = mask.shape[1], arrays[0].shape[1]
    half = tokens // 2
    outer = len(weights)
    made = [jax.ShapeDtypeStruct((GROUP, half, width), BF)] * 2
    made += [jax.ShapeDtypeStruct((GROUP, tokens, HEAD_DIM), BF)] * 4
    return pl.pallas_call(
        functools.partial(attend_kernel, moves, shard_rows, outer),
        grid_spec=pltpu.PrefetchScalarGridSpec(
            num_scalar_prefetch=1,
            grid=(GROUP,),
            in_specs=row_specs(tokens) + [ANYWHERE] * (outer + len(arrays)),
            out_specs=[stepped(half, width)] * 2 + [stepped(tokens, HEAD_DIM)] * 4,
            scratch_shapes=[
                pltpu.VMEM((GROUP, tokens, width), BF),
                pltpu.VMEM((outer * GROUP, *weights[0].shape[1:]), BF),
                pltpu.SemaphoreType.DMA((len(arrays),)),
                pltpu.SemaphoreType.DMA((outer,)),
            ],
        ),
        out_shape=made,
        compiler_params=params(),
        cost_estimate=pl.CostEstimate(
            flops=2 * GROUP * tokens * (width * 4 + 2 * tokens) * HEAD_DIM,
            bytes_accessed=4 * GROUP * tokens * width,
            transcendentals=GROUP * tokens * tokens,
        ),
        name="attend",
    )(places, cosine, sine, mask, *weights, *arrays)


def feed_kernel(moves, cot_moves, outer, places, *refs):
    weights, refs = refs[:outer], refs[outer:]
    count, cot_count = len(moves), len(cot_moves)
    pieces, cots, refs = refs[:count], refs[count : count + cot_count], refs[count + cot_count :]
    m_own, m_other, hidden_ref, gate_ref, upper_ref, *refs = refs
    held, held_cot, weight, sems, cot_sems, weight_sems = refs
    step = pl.program_id(0)
    wait = fetch_weights(weights, weight, weight_sems, step)
    fetch(moves, pieces, held, sems, step)
    fetch(cot_moves, cots, held_cot, cot_sems, step)
    wait()
    width = held.shape[2]
    own = weight.shape[3]
    rows = held[step]
    half = rows.shape[0] // 2
    gate_w = weight[:, 0].reshape(width, own)
    upper_w = weight[:, 1].reshape(width, own)
    down_w = weight[:, 2].reshape(width, own)
    gate = dot(rows, gate_w, 1, 0)
    upper = dot(rows, upper_w, 1, 0)
    grad_hidden = dot(held_cot[step], down_w, 1, 0)
    sigma = 1.0 / (1.0 + jnp.exp(-gate))
    silu = gate * sigma
    hidden = (silu * upper).astype(BF)
    grad_gate = (grad_hidden * upper * (sigma * (1.0 + gate * (1.0 - sigma)))).astype(BF)
    grad_upper = (grad_hidden * silu).astype(BF)
    hidden_ref[0], gate_ref[0], upper_ref[0] = hidden, grad_gate, grad_upper
    back = (dot(grad_gate, gate_w, 1, 1) + dot(grad_upper, upper_w, 1, 1)).astype(BF)
    m_own[0, :half], m_other[0, :half] = back[:half], back[half:]
    out = dot(hidden, down_w, 1, 1).astype(BF)
    m_own[0, half:], m_other[0, half:] = out[:half], out[half:]


def feed(places, weights, rows_two, rows_cot, rows):
    (arrays, moves), (cot_arrays, cot_moves) = rows_two, rows_cot
    half, width = rows, arrays[0].shape[1]
    outer = len(weights)
    tokens, own = 2 * half, weights[0].shape[3]
    made = [jax.ShapeDtypeStruct((GROUP, tokens, width), BF)] * 2
    made += [jax.ShapeDtypeStruct((GROUP, tokens, own), BF)] * 3
    return pl.pallas_call(
        functools.partial(feed_kernel, moves, cot_moves, outer),
        grid_spec=pltpu.PrefetchScalarGridSpec(
            num_scalar_prefetch=1,
            grid=(GROUP,),
            in_specs=[ANYWHERE] * (outer + len(arrays) + len(cot_arrays)),
            out_specs=[stepped(tokens, width)] * 2 + [stepped(tokens, own)] * 3,
            scratch_shapes=[
                pltpu.VMEM((GROUP, tokens, width), BF),
                pltpu.VMEM((GROUP, tokens, width), BF),
                pltpu.VMEM((outer * GROUP, *weights[0].shape[1:]), BF),
                pltpu.SemaphoreType.DMA((len(arrays),)),
                pltpu.SemaphoreType.DMA((len(cot_arrays),)),
                pltpu.SemaphoreType.DMA((outer,)),
            ],
        ),
        out_shape=made,
        compiler_params=params(),
        cost_estimate=pl.CostEstimate(
            flops=12 * GROUP * tokens * width * own,
            bytes_accessed=8 * GROUP * tokens * width,
            transcendentals=GROUP * tokens * own,
        ),
        name="feed",
    )(places, *weights, *arrays, *cot_arrays)


def grads_kernel(layout, count_rights, places, *refs):
    count = len(layout)
    pieces, refs = refs[:count], refs[count:]
    rights, (*_, out, held, sems) = refs[:count_rights], refs[count_rights:]
    step, which = pl.program_id(0), pl.program_id(1)

    @pl.when((step == 0) & (which == 0))
    def _():
        copies = moves_of(layout, pieces, held, sems)
        for _, copy in copies:
            copy.start()
        for _, copy in copies:
            copy.wait()

    shards, _, rows, own = out.shape
    tile = shards * rows
    tokens = held.shape[0] * held.shape[1]
    for i, right in enumerate(rights):

        @pl.when(which == i)
        def _():
            left = held[:, :, pl.ds(pl.multiple_of(step * tile, 128), tile)].reshape(tokens, tile)
            product = dot(left, right[...].reshape(tokens, own), 0, 0)
            out[:, 0] = product.astype(BF).reshape(shards, rows, own)


def by_group(step, places):
    return 2 * ((step // 2) ^ places[GROUP]) + step % 2


def by_place(step, places):
    group = (step // 2) ^ places[GROUP]
    return 4 * (group // 2) + 2 * (step % 2) + group % 2


def weight_grads(places, pieces, rights, shard_rows, order, shape, at, into=None):
    arrays, layout = pieces
    _, tokens, own = rights[0].shape
    width = arrays[0].shape[1]
    tile = GROUP * shard_rows // 2
    kept = [] if into is None else [into]
    made = jax.ShapeDtypeStruct((width // shard_rows, shape[0], shard_rows, shape[1]), BF)
    return pl.pallas_call(
        functools.partial(grads_kernel, layout, len(rights)),
        grid_spec=pltpu.PrefetchScalarGridSpec(
            num_scalar_prefetch=1,
            grid=(width // tile, len(rights)),
            in_specs=[ANYWHERE] * len(arrays)
            + [
                pl.BlockSpec(right.shape, lambda step, which, places: (0, 0, 0))
                for right in rights
            ]
            + [ANYWHERE] * len(kept),
            out_specs=pl.BlockSpec(
                (tile // shard_rows, 1, shard_rows, own),
                lambda step, which, places: (order(step, places), at[0] + which, 0, at[1]),
            ),
            scratch_shapes=[
                pltpu.VMEM((GROUP, tokens, width), BF),
                pltpu.SemaphoreType.DMA((len(arrays),)),
            ],
        ),
        out_shape=made,
        input_output_aliases={1 + len(arrays) + len(rights): 0} if kept else {},
        compiler_params=pltpu.CompilerParams(
            dimension_semantics=("arbitrary", "arbitrary"), vmem_limit_bytes=VMEM_LIMIT
        ),
        cost_estimate=pl.CostEstimate(
            flops=2 * GROUP * tokens * width * own * len(rights),
            bytes_accessed=2 * GROUP * tokens * width,
            transcendentals=0,
        ),
        name="weight_grads",
    )(places, *arrays, *rights, *kept)


def pack_heads_kernel(qkv, out_weight, gain, note, packed):
    rows, columns = out_weight.shape
    for member in range(GROUP):
        for which in range(3):
            first = which * columns + member * HEAD_DIM
            part = qkv[:, first : first + HEAD_DIM].astype(F32) * gain[...]
            packed[member, :rows, which * HEAD_DIM : (which + 1) * HEAD_DIM] = part.astype(BF)
        first = member * HEAD_DIM
        packed[member, :rows, 3 * HEAD_DIM :] = out_weight[:, first : first + HEAD_DIM]
        packed[member, rows:, :] = note[...]


def pack_feed_kernel(gate_up, down, gain, packed):
    own = packed.shape[3]
    for which in range(3):
        for member in range(GROUP):
            if which < 2:
                first = (which * GROUP + member) * own
                part = (gate_up[:, first : first + own].astype(F32) * gain[...]).astype(BF)
            else:
                part = down[:, member * own : (member + 1) * own]
            packed[member, which] = part


def gained(gain_ref, sums):
    total = sum(jnp.sum(part, axis=1, keepdims=True) for part in sums)
    gain_ref[...] = jnp.broadcast_to(total, gain_ref.shape)


def unpack_heads_kernel(sources, got, qkv, gain, qkv_ref, out_ref, gain_ref):
    columns = out_ref.shape[1]
    sums = []
    for member in range(GROUP):
        total = sum(got[source].astype(F32) for source in sources[member])
        for which in range(3):
            first = which * columns + member * HEAD_DIM
            part = total[:, which * HEAD_DIM : (which + 1) * HEAD_DIM]
            sums.append(qkv[:, first : first + HEAD_DIM].astype(F32) * part)
            qkv_ref[:, first : first + HEAD_DIM] = part * gain[...]
        out_ref[:, member * HEAD_DIM : (member + 1) * HEAD_DIM] = total[:, 3 * HEAD_DIM :]
    gained(gain_ref, sums)


def unpack_feed_kernel(got, gate_up, gain, gate_up_ref, down_ref, gain_ref):
    own = got.shape[3]
    sums = []
    for which in range(3):
        for member in range(GROUP):
            part = got[member, which].astype(F32)
            if which < 2:
                first = (which * GROUP + member) * own
                sums.append(gate_up[:, first : first + own].astype(F32) * part)
                gate_up_ref[:, first : first + own] = part * gain[...]
            else:
                down_ref[:, member * own : (member + 1) * own] = part
    gained(gain_ref, sums)


def plain_call(kernel, name, arrays, made):
    in_vmem = pl.BlockSpec(memory_space=pltpu.VMEM)
    return pl.pallas_call(
        kernel,
        in_specs=[in_vmem] * len(arrays),
        out_specs=jax.tree.map(lambda _: in_vmem, made),
        out_shape=made,
        compiler_params=pltpu.CompilerParams(vmem_limit_bytes=VMEM_LIMIT),
        name=name,
    )(*arrays)


def attend_back_kernel(
    moves, shard_rows, outer, places, cosine, sine, mask, q_ref, k_ref, v_ref, *refs
):
    weights, refs = refs[:outer], refs[outer:]
    count = len(moves)
    pieces, refs = refs[:count], refs[count:]
    grad_ref, m_own, m_other, held, weight, sems, weight_sems = refs
    step = pl.program_id(0)
    wait = fetch_weights(weights, weight, weight_sems, step)
    fetch(moves, pieces, held, sems, step)
    wait()
    qkv_w, out_w = head_weights(weight, shard_rows)
    queries, keys, values = q_ref[0], k_ref[0], v_ref[0]
    grad_mixed = dot(held[step], out_w, 1, 0).astype(BF)
    probs = probabilities(queries, keys, mask[0])
    grad_values = dot(probs.astype(BF), grad_mixed, 0, 0)
    grad_probs = dot(grad_mixed, values, 1, 1)
    delta = jnp.sum(probs * grad_probs, axis=1, keepdims=True)
    grad_scores = (probs * (grad_probs - delta) * (HEAD_DIM**-0.5)).astype(BF)
    grad_queries = turned(dot(grad_scores, keys, 1, 0), cosine[0], -sine[0])
    grad_keys = turned(dot(grad_scores, queries, 0, 0), cosine[0], -sine[0])
    grads = jnp.concatenate([grad_queries, grad_keys, grad_values], axis=1).astype(BF)
    grad_ref[0] = grads
    back = dot(grads, qkv_w, 1, 1).astype(BF)
    half = back.shape[0] // 2
    m_own[0], m_other[0] = back[:half], back[half:]


def attend_back(places, rows_grad, weights, shard_rows, cosine, sine, mask, queries, keys, values):
    arrays, moves = rows_grad
    tokens, width = mask.shape[1], arrays[0].shape[1]
    half = tokens // 2
    outer = len(weights)
    made = [jax.ShapeDtypeStruct((GROUP, tokens, 3 * HEAD_DIM), BF)]
    made += [jax.ShapeDtypeStruct((GROUP, half, width), BF)] * 2
    return pl.pallas_call(
        functools.partial(attend_back_kernel, moves, shard_rows, outer),
        grid_spec=pltpu.PrefetchScalarGridSpec(
            num_scalar_prefetch=1,
            grid=(GROUP,),
            in_specs=row_specs(tokens)
            + [stepped(tokens, HEAD_DIM)] * 3
            + [ANYWHERE] * (outer + len(arrays)),
            out_specs=[stepped(tokens, 3 * HEAD_DIM)] + [stepped(half, width)] * 2,
            scratch_shapes=[
                pltpu.VMEM((GROUP, tokens, width), BF),
                pltpu.VMEM((outer * GROUP, *weights[0].shape[1:]), BF),
                pltpu.SemaphoreType.DMA((len(arrays),)),
                pltpu.SemaphoreType.DMA((outer,)),
            ],
        ),
        out_shape=made,
        compiler_params=params(),
        cost_estimate=pl.CostEstimate(
            flops=2 * GROUP * tokens * (width * 4 + 5 * tokens) * HEAD_DIM,
            bytes_accessed=4 * GROUP * tokens * width,
            transcendentals=GROUP * tokens * tokens,
        ),
        name="attend_back",
    )(places, cosine, sine, mask, queries, keys, values, *weights, *arrays)


def doc_layout(lengths, positions):
    docs = jnp.arange(lengths.shape[1], dtype=jnp.int32)
    ends_at = jnp.sum(
        jnp.where(docs[None, None, :] <= docs[None, :, None], lengths[:, None, :], 0),
        axis=2,
        dtype=jnp.int32,
    )
    passed = positions[None, :, None] >= ends_at[:, None, :]
    segment = jnp.sum(passed.astype(jnp.int32), axis=2, dtype=jnp.int32)
    doc_start = jnp.sum(jnp.where(passed, lengths[:, None, :], 0), axis=2, dtype=jnp.int32)
    offset = (positions[None, :] - doc_start).astype(F32)
    allowed = (segment[:, :, None] == segment[:, None, :]) & (
        positions[None, :, None] >= positions[None, None, :]
    )
    half_dim = HEAD_DIM // 2
    inverse = jnp.exp(
        jnp.arange(half_dim, dtype=F32) * (-2.0 * math.log(10000.0) / HEAD_DIM)
    )
    angles = offset[:, :, None] * inverse
    cosine, sine = jnp.cos(angles), jnp.sin(angles)
    return (
        allowed.astype(BF),
        jnp.concatenate([cosine, cosine], axis=2),
        jnp.concatenate([-sine, sine], axis=2),
    )


def rms_scale(values):
    return lax.rsqrt(jnp.mean(values * values, axis=-1, keepdims=True) + EPS_NORM)


def norm_back(grad_normed, normed, scale):
    return scale * (
        grad_normed - normed * jnp.mean(grad_normed * normed, axis=-1, keepdims=True)
    )


def shards(
    tokens,
    norm1_gain,
    qkv_weight,
    out_weight,
    norm2_gain,
    gate_up_weight,
    down_weight,
    doc_lengths,
    cotangent,
):
    rows, width = tokens.shape
    place = lax.axis_index("dp")
    core = lax.axis_index("tensor")
    member = place % NEXT + NEXT * ((place // Z) % 2)
    group = (place // NEXT) % 2 + 2 * (place // (2 * Z))
    outer = lax.axis_size("dp") // GROUP
    row_count = 2 * rows
    shard_rows, _, local_width = qkv_weight.shape
    own_hidden = gate_up_weight.shape[2] // GROUP
    assert local_width == GROUP * HEAD_DIM
    places = jnp.concatenate(
        [jnp.array(ORDER, jnp.int32) ^ member, jnp.reshape(group, (1,)).astype(jnp.int32)]
    )

    def rolled(x):
        shaped = x.reshape(rows, outer // 2, 2, 2, NEXT * shard_rows)
        return flip_blocks(jnp.swapaxes(shaped, 2, 3).reshape(x.shape), 1, outer, group)

    def unrolled(x):
        shaped = flip_blocks(x, 1, outer, group).reshape(rows, outer // 2, 2, 2, NEXT * shard_rows)
        return jnp.swapaxes(shaped, 2, 3).reshape(x.shape)

    gain_one = norm1_gain.astype(F32)[:, None]
    gain_two = norm2_gain.astype(F32)[:, None]

    residual = rolled(tokens).astype(F32)
    scale_one = rms_scale(residual)
    normed_one = residual * scale_one
    blocks_one = gather(normed_one.astype(BF))
    rows_one = part_of(with_other_core(blocks_one), 0, rows)
    qkv_flat = qkv_weight.reshape(shard_rows, 3 * local_width)
    docs = doc_lengths.shape[1]
    note = jnp.pad(doc_lengths.astype(BF), ((0, 15), (0, 4 * HEAD_DIM - docs)))
    head_own = swap_members(
        plain_call(
            pack_heads_kernel,
            "pack_heads",
            [qkv_flat, out_weight, gain_one, note],
            jax.ShapeDtypeStruct((GROUP, shard_rows + 16, 4 * HEAD_DIM), BF),
        )
    )
    head_mats = outer_gather(head_own)
    chosen = (jnp.arange(GROUP, dtype=jnp.int32)[None, :] == places[:GROUP, None])[:, :, None]
    lengths = jnp.sum(
        jnp.where(chosen, head_own[:, shard_rows, :docs].astype(F32)[None], 0.0), axis=1
    ).astype(jnp.int32)
    positions = (jnp.arange(row_count, dtype=jnp.int32) + rows * core) % row_count
    mask, cosine, sine = doc_layout(lengths, positions)

    gate_up_flat = gate_up_weight.reshape(shard_rows, 2 * GROUP * own_hidden)
    feed_packed = plain_call(
        pack_feed_kernel,
        "pack_feed",
        [gate_up_flat, down_weight, gain_two],
        jax.ShapeDtypeStruct((GROUP, 3, shard_rows, own_hidden), BF),
    )
    feed_mats = outer_gather(swap_members(after(feed_packed, blocks_one[1])))
    cot_own = rolled(cotangent)
    blocks_cot = gather(after(cot_own, *blocks_one[4:]))
    rows_cot = part_of(with_other_core(blocks_cot), 0, rows)

    a_own, a_other, mixed, queries, keys, values = attend(
        places, rows_one, head_mats, shard_rows, cosine, sine, mask
    )
    attn_blocks = after_all(both_cores(a_own, a_other), *blocks_cot[1:3])
    attn = reduce_last(*reduce_second(reduce_first(attn_blocks)))
    stream = residual + attn
    scale_two = rms_scale(stream)
    normed_two = stream * scale_two
    blocks_two = gather(after(normed_two.astype(BF), *blocks_cot[4:]))
    rows_two = part_of(with_other_core(blocks_two), 0, rows)

    m_own, m_other, hidden, grad_gate, grad_upper = feed(
        places, feed_mats, rows_two, rows_cot, rows
    )
    feed_shape = (3, own_hidden)
    feed_part = weight_grads(
        places, rows_cot, [hidden], shard_rows, by_group, feed_shape, (2, 0)
    )
    ends = both_cores(m_own, m_other)
    first = reduce_first(ends)
    second = reduce_second(after_all(first, feed_part))
    feed_part = weight_grads(
        places,
        rows_two,
        after_all([grad_gate, grad_upper], *first),
        shard_rows,
        by_group,
        feed_shape,
        (0, 0),
        feed_part,
    )
    both = reduce_last(*after_all(second, feed_part))
    back_two, mlp_out = both[:rows], both[rows:]
    feed_sum = outer_reduce(feed_part)
    feed_got = swap_members(feed_sum)
    grad_stream = cot_own.astype(F32) + norm_back(back_two, normed_two, scale_two)

    grad_low = grad_stream.astype(BF)
    rows_grad = part_of(with_other_core(gather(grad_low)), 0, rows)
    grad_qkv, m_own, m_other = attend_back(
        places,
        rows_grad,
        head_mats,
        shard_rows,
        cosine,
        sine,
        after(mask, feed_sum),
        queries,
        keys,
        values,
    )
    head_shape = (1, 4 * HEAD_DIM)
    head_part = weight_grads(
        places, rows_grad, [mixed], shard_rows, by_place, head_shape, (0, 3)
    )
    head_part = weight_grads(
        places, rows_one, [grad_qkv], shard_rows, by_place, head_shape, (0, 0), head_part
    )
    head_got = lax.all_to_all(head_part[:, 0], "dp", split_axis=0, concat_axis=0, tiled=True)
    ends = after_all(both_cores(m_own, m_other), head_part)
    back_one = reduce_last(*reduce_second(reduce_first(ends)))

    output = unrolled((stream + mlp_out).astype(BF))
    input_grad = unrolled((grad_stream + norm_back(back_one, normed_one, scale_one)).astype(BF))
    gate_up_grad, down_grad, gain_two_part = plain_call(
        unpack_feed_kernel,
        "unpack_feed",
        [feed_got, gate_up_flat, gain_two],
        [
            jax.ShapeDtypeStruct(gate_up_flat.shape, F32),
            jax.ShapeDtypeStruct(down_weight.shape, F32),
            jax.ShapeDtypeStruct((shard_rows, 128), F32),
        ],
    )
    sources = [
        [
            16 * (other // 2) + Z * (one // NEXT) + NEXT * (other % 2) + one % NEXT
            for other in range(outer)
        ]
        for one in range(GROUP)
    ]
    qkv_grad, out_grad, gain_one_part = plain_call(
        functools.partial(unpack_heads_kernel, sources),
        "unpack_heads",
        [head_got, qkv_flat, gain_one],
        [
            jax.ShapeDtypeStruct(qkv_flat.shape, F32),
            jax.ShapeDtypeStruct(out_weight.shape, F32),
            jax.ShapeDtypeStruct((shard_rows, 128), F32),
        ],
    )
    gain_two_part, gain_one_part = gain_two_part[:, 0], gain_one_part[:, 0]
    return (
        output,
        input_grad,
        gain_one_part + over_cores(gain_one_part),
        qkv_grad.reshape(qkv_weight.shape),
        out_grad,
        gain_two_part + over_cores(gain_two_part),
        gate_up_grad.reshape(gate_up_weight.shape),
        down_grad,
    )


def solution(mesh):
    placed = (
        P(("dp", "tensor"), None),
        P("dp"),
        P("dp", None, "tensor"),
        P("dp", "tensor"),
        P("dp"),
        P("dp", None, "tensor"),
        P("dp", "tensor"),
        P("dp", None),
        P(("dp", "tensor"), None),
    )
    return jax.shard_map(
        shards,
        mesh=mesh,
        in_specs=placed,
        out_specs=(
            P(("dp", "tensor"), None),
            P(("dp", "tensor"), None),
            P("dp"),
            P("dp", None, "tensor"),
            P("dp", "tensor"),
            P("dp"),
            P("dp", None, "tensor"),
            P("dp", "tensor"),
        ),
        check_vma=False,
    )
```

time: 936 us -> 758 us (0.81)
  local copies, waits for them, and re-layouts: 214 us -> 58.4 us
  Pallas kernels: 0 us -> 147 us
  matrix products: 105 us -> 0 us
  waiting for transfers between devices: 402 us -> 361 us
  starting transfers between devices: 140 us -> 108 us
  other arithmetic: 58.4 us -> 69.9 us
    pallas_call x0 -> x11, Pallas kernels: none -> 147 us  [the longest x4 50.8 us: weight_grads(): pl.pallas_call(functools.partial(grads_kernel, layout, len(rights)), grid...]
    dot_general x19 -> x0, matrix products: 101 us -> none  [dot(): lax.dot_general(left, right, (contract, batch), preferred_element_type=F32)]
    unnamed x253 -> x111, local copies, waits for them, and re-layouts: 93.7 us -> 14.8 us
    ppermute x97 -> x51, waiting for transfers between devices: 402 us -> 341 us  [over_dp(): return lax.ppermute(x, 'dp', [(i, i ^ bit) for i in range(size)])]
    concatenate x8 -> x1, local copies, waits for them, and re-layouts: 59.8 us -> 0.21 us  [flip_blocks(): jnp.concatenate([lax.slice_in_dim(view, 1, 2, axis=axis + 1), lax.slice_i...]
    slice x35 -> x2, local copies, waits for them, and re-layouts: 35.5 us -> 1.88 us  [shards(): gain_two_part, gain_one_part = (gain_two_part[:, 0], gain_one_part[:, 0])]
    convert_element_type x3 -> x11, other arithmetic: 3.86 us -> 36.1 us  [plus(): return (base.astype(F32) + more.astype(F32)).astype(BF)]
    ppermute x97 -> x51, starting transfers between devices: 96.4 us -> 66 us  [over_dp(): return lax.ppermute(x, 'dp', [(i, i ^ bit) for i in range(size)])]
  transfers between devices with their start and end apart: 151 -> 93, of which waited for: 54 -> 37; matrix products, arithmetic and copies ran while one was open for 33% -> 11% of each run, Pallas kernels for 0% -> 12%
where the time goes in v3:
time: 758 us; the launch traced here: 746 us
  waiting for transfers between devices  361 us (48%)
  Pallas kernels  147 us (19%)
  starting transfers between devices  108 us (14%)
  other arithmetic  69.9 us (9%)
  local copies, waits for them, and re-layouts  58.4 us (8%)
    ppermute x51, waiting for transfers between devices, over_dp(): return lax.ppermute(x, 'dp', [(i, i ^ bit) for i in range(size)])  341 us
    ppermute x51, starting transfers between devices, over_dp(): return lax.ppermute(x, 'dp', [(i, i ^ bit) for i in range(size)])  66 us
    pallas_call x4, Pallas kernels, weight_grads(): pl.pallas_call(functools.partial(grads_kernel, layout, len(rights)), grid...  50.8 us
    pallas_call x1, Pallas kernels, feed(): pl.pallas_call(functools.partial(feed_kernel, moves, cot_moves, outer), g...  36.6 us
    convert_element_type x11, other arithmetic, plus(): return (base.astype(F32) + more.astype(F32)).astype(BF)  36.1 us
    pallas_call x1, Pallas kernels, attend_back(): pl.pallas_call(functools.partial(attend_back_kernel, moves, shard_rows, o...  20.8 us
    pallas_call x1, Pallas kernels, attend(): pl.pallas_call(functools.partial(attend_kernel, moves, shard_rows, outer)...  20.7 us
    all_to_all x3, starting transfers between devices, swap_members(): lax.all_to_all(blocks, 'dp', split_axis=0, concat_axis=0, tiled=True, axi...  18.8 us
  transfers between devices with their start and end apart: 93, of which 37 were waited for; matrix products, arithmetic and copies ran while one was open for 11% of the time, Pallas kernels for 12%

profile of v3, /device:TPU:24, one launch (start us, length us, event | category | flops | bytes accessed | tf_op | source)
XLA Modules:
  0.0 745.7 jit_solution(3078640234881524309)
XLA Ops:
  22.1 41.0 %collective-permute-done.6.refs_8_.refs_6_ = bf16[128,2048]{1,0:T(8,128)(2,1)S(1)} collective-permute-done((bf16[128,2048]{1,0:T(8,128)(2,1)S(1)}, bf16[128,2048]{1,0:T(8,128)(2,1)S(1)}, u32[]{:S(2)}, u32[]{:S(2)}) %collective-permute-start.6) | collective-permute-done | bytes 524320 | tf_op jit(solution)/shard_map/ppermute | solution.py:25
  68.3 8.7 %collective-permute-done.12.refs_14_.refs_12_ = bf16[128,2048]{1,0:T(8,128)(2,1)S(1)} collective-permute-done((bf16[128,2048]{1,0:T(8,128)(2,1)S(1)}, bf16[128,2048]{1,0:T(8,128)(2,1)S(1)}, u32[]{:S(2)}, u32[]{:S(2)}) %collective-permute-start.12) | collective-permute-done | bytes 524320 | tf_op jit(solution)/shard_map/ppermute | solution.py:25
  100.2 20.7 %attend.1 = (bf16[8,128,2048]{2,1,0:T(8,128)(2,1)}, bf16[8,128,2048]{2,1,0:T(8,128)(2,1)}, bf16[8,256,128]{2,1,0:T(8,128)(2,1)}, bf16[8,256,128]{2,1,0:T(8,128)(...) custom-call(s32[9]{0:T(128)} %pad_add_fusion.places, f32[8,256,128]{2,1,0:T(8,128)} %pad_maximum_fusion.cosine, ...), custom_call_target="tpu_custom_call" | custom-call | flops 4563402752 | bytes 16777216 | tf_op jit(solution)/shard_map/attend/pallas_call | solution.py:269
  150.8 12.6 %collective-permute-done.18.refs_22_.refs_4_ = bf16[128,2048]{1,0:T(8,128)(2,1)S(1)} collective-permute-done((bf16[128,2048]{1,0:T(8,128)(2,1)}, bf16[128,2048]{1,0:T(8,128)(2,1)S(1)}, u32[]{:S(2)}, u32[]{:S(2)}) %collective-permute-start.18) | collective-permute-done | bytes 524320 | tf_op jit(solution)/shard_map/ppermute | solution.py:25
  167.8 10.5 %collective-permute-start.28 = (bf16[128,2048]{1,0:T(8,128)(2,1)}, bf16[128,2048]{1,0:T(8,128)(2,1)}, u32[]{:S(2)}, u32[]{:S(2)}) collective-permute-start(bf16[128,2048]{1,0:T(8,128)(2,1)} %broadcast_select_fusion.refs_18_.refs_0_), channel_id=1, source_target_pairs={{0,16},{2,18},{4,20},{6,22},{8,24},{10,26},{12,28},{14,30},{16,0},... | collective-permute-start | bytes 1572872 | tf_op jit(solution)/shard_map/ppermute | solution.py:25
  190.1 18.3 %collective-permute-done.28.refs_24_.refs_6_ = bf16[128,2048]{1,0:T(8,128)(2,1)} collective-permute-done((bf16[128,2048]{1,0:T(8,128)(2,1)}, bf16[128,2048]{1,0:T(8,128)(2,1)}, u32[]{:S(2)}, u32[]{:S(2)}) %collective-permute-start.28) | collective-permute-done | bytes 524320 | tf_op jit(solution)/shard_map/ppermute | solution.py:25
  212.7 10.8 %collective-permute-done.29.refs_28_.refs_10_ = bf16[128,2048]{1,0:T(8,128)(2,1)} collective-permute-done((bf16[128,2048]{1,0:T(8,128)(2,1)}, bf16[128,2048]{1,0:T(8,128)(2,1)}, u32[]{:S(2)}, u32[]{:S(2)}) %collective-permute-start.29) | collective-permute-done | bytes 524320 | tf_op jit(solution)/shard_map/ppermute | solution.py:25
  252.4 42.2 %collective-permute-done.37.refs_8_.refs_6_ = bf16[128,2048]{1,0:T(8,128)(2,1)S(1)} collective-permute-done((bf16[128,2048]{1,0:T(8,128)(2,1)S(1)}, bf16[128,2048]{1,0:T(8,128)(2,1)S(1)}, u32[]{:S(2)}, u32[]{:S(2)}) %collective-permute-start.37) | collective-permute-done | bytes 524320 | tf_op jit(solution)/shard_map/ppermute | solution.py:25
  299.3 10.3 %collective-permute-done.41.refs_12_.refs_10_ = bf16[128,2048]{1,0:T(8,128)(2,1)} collective-permute-done((bf16[128,2048]{1,0:T(8,128)(2,1)S(1)}, bf16[128,2048]{1,0:T(8,128)(2,1)}, u32[]{:S(2)}, u32[]{:S(2)}) %collective-permute-start.41) | collective-permute-done | bytes 524320 | tf_op jit(solution)/shard_map/ppermute | solution.py:25
  326.7 36.6 %feed.1 = (bf16[8,256,2048]{2,1,0:T(8,128)(2,1)}, bf16[8,256,2048]{2,1,0:T(8,128)(2,1)}, bf16[8,256,352]{2,1,0:T(8,128)(2,1)}, bf16[8,256,352]{2,1,0:T(8,128)(2,1)}, bf16[8,256,352]{2,1,0:T(8,128)(2,1)}) custom-call(s32[9]{0:T(128)} %pad_add_fusion.places, bf16[8,3,128,352]{3,2,1,0:T(8,128)(2,1)} %copy.148.refs_0_, bf16[8,3,128,352]{3,2,1,0:T(8,128)(2,1)} %copy.149.refs_1_, ...), custom_call_target="tpu_custom_call" | custom-call | flops 17716740096 | bytes 33554432 | tf_op jit(solution)/shard_map/feed/pallas_call | solution.py:334
  363.8 13.0 %collective-permute-done.55 = bf16[8,256,2048]{2,1,0:T(8,128)(2,1)S(1)} collective-permute-done((bf16[8,256,2048]{2,1,0:T(8,128)(2,1)}, bf16[8,256,2048]{2,1,0:T(8,128)(2,1)S(1)}, u32[]{:S(2)}, u32[]{:S(2)}) %collective-permute-start.55) | collective-permute-done | bytes 8388640 | tf_op jit(solution)/shard_map/ppermute | solution.py:29
  376.8 15.3 %fusion.18 = (bf16[256,2048]{1,0:T(8,128)(2,1)}, bf16[256,2048]{1,0:T(8,128)(2,1)}, bf16[256,2048]{1,0:T(8,128)(2,1)}, bf16[256,2048]{1,0:T(8,128)(2,1)}, bf16[256,2048]{1,0:T(8,128)(2,1)}) fusion(bf16[8,256,2048]{2,1,0:T(8,128)(2,1)S(1)} %collective-permute-done.55, bf16[8,256,2048]{2,1,0:T(8,128)(2,1)} %get-tuple-element.72), kind=kLoop, calls=%fused_computation.36 | loop fusion | flops 10485760 | bytes 15728640 | tf_op jit(solution)/shard_map/convert_element_type | solution.py:88
  394.9 11.8 %weight_grads.4.refs_18_ = bf16[16,3,128,352]{3,2,1,0:T(8,128)(2,1)} custom-call(s32[9]{0:T(128)} %pad_add_fusion.places, bf16[128,2048]{1,0:T(8,128)(2,1)} %broadcast_select_fusion.refs_18_.refs_0_, bf16[128,2048]{1,0:T(8,128)(2,1)} %collective-permute-done.47.refs_19_.refs_1_, bf16[128,2048]{1,0:T(8,128)(2,1)} %collective-permute-done.17.refs_20_.refs_2_, ...), custom_call_target="tpu_custom_call" | custom-call | flops 2952790016 | bytes 8388608 | tf_op jit(solution)/shard_map/weight_grads/pallas_call | solution.py:403
  406.7 11.7 %collective-permute-done.58 = bf16[256,2048]{1,0:T(8,128)(2,1)S(1)} collective-permute-done((bf16[256,2048]{1,0:T(8,128)(2,1)}, bf16[256,2048]{1,0:T(8,128)(2,1)S(1)}, u32[]{:S(2)}, u32[]{:S(2)}) %collective-permute-start.58) | collective-permute-done | bytes 1048608 | tf_op jit(solution)/shard_map/ppermute | solution.py:25
  418.4 21.9 %collective-permute-done.57 = bf16[256,2048]{1,0:T(8,128)(2,1)S(1)} collective-permute-done((bf16[256,2048]{1,0:T(8,128)(2,1)}, bf16[256,2048]{1,0:T(8,128)(2,1)S(1)}, u32[]{:S(2)}, u32[]{:S(2)}) %collective-permute-start.57) | collective-permute-done | bytes 1048608 | tf_op jit(solution)/shard_map/ppermute | solution.py:25
  448.8 17.8 %weight_grads.5 = bf16[16,3,128,352]{3,2,1,0:T(8,128)(2,1)} custom-call(s32[9]{0:T(128)} %pad_add_fusion.places, bf16[128,2048]{1,0:T(8,128)(2,1)} %copy-done.41, bf16[128,2048]{1,0:T(8,128)(2,1)} %copy-done.47, bf16[128,2048]{1,0:T(8,128)(2,1)} %collective-permute-done.33.refs_4_.refs_2_, ...), custom_call_target="tpu_custom_call", output_to_operand_aliasing={{}: (19, {})} | custom-call | flops 5905580032 | bytes 8388608 | tf_op jit(solution)/shard_map/weight_grads/pallas_call | solution.py:403
  500.3 24.2 %collective-permute-done.62 = bf16[256,2048]{1,0:T(8,128)(2,1)} collective-permute-done((bf16[256,2048]{1,0:T(8,128)(2,1)}, bf16[256,2048]{1,0:T(8,128)(2,1)}, u32[]{:S(2)}, u32[]{:S(2)}) %collective-permute-start.62) | collective-permute-done | bytes 1048608 | tf_op jit(solution)/shard_map/ppermute | solution.py:25
  532.0 26.8 %collective-permute-done.68.refs_8_.refs_6_ = bf16[128,2048]{1,0:T(8,128)(2,1)S(1)} collective-permute-done((bf16[128,2048]{1,0:T(8,128)(2,1)S(1)}, bf16[128,2048]{1,0:T(8,128)(2,1)S(1)}, u32[]{:S(2)}, u32[]{:S(2)}) %collective-permute-start.68) | collective-permute-done | bytes 524320 | tf_op jit(solution)/shard_map/ppermute | solution.py:25
  562.9 10.9 %collective-permute-done.72.refs_12_.refs_10_ = bf16[128,2048]{1,0:T(8,128)(2,1)} collective-permute-done((bf16[128,2048]{1,0:T(8,128)(2,1)S(1)}, bf16[128,2048]{1,0:T(8,128)(2,1)}, u32[]{:S(2)}, u32[]{:S(2)}) %collective-permute-start.72) | collective-permute-done | bytes 524320 | tf_op jit(solution)/shard_map/ppermute | solution.py:25
  596.0 20.8 %attend_back.1 = (bf16[8,256,384]{2,1,0:T(8,128)(2,1)}, bf16[8,128,2048]{2,1,0:T(8,128)(2,1)}, bf16[8,128,2048]{2,1,0:T(8,128)(2,1)}) custom-call(s32[9]{0:T(128)} %pad_add_fusion.places, f32[8,256,128]{2,1,0:T(8,128)} %pad_maximum_fusion.cosine, f32[8,256,128]{2,1,0:T(8,128)} %pad_maximum_fusion.1.sine, bf16[8,256,256]{2,1,0:T(8,128)(2,1)} %and_convert_fusion.mask, ...), custom_call_target="tpu_custom_call" | custom-call | flops 4966055936 | bytes 16777216 | tf_op jit(solution)/shard_map/attend_back/pallas_call | solution.py:542
  617.1 9.4 %weight_grads.6.refs_17_ = bf16[16,1,128,512]{3,2,1,0:T(8,128)(2,1)} custom-call(s32[9]{0:T(128)} %pad_add_fusion.places, bf16[128,2048]{1,0:T(8,128)(2,1)} %copy-done.7, bf16[128,2048]{1,0:T(8,128)(2,1)} %copy-done.36, bf16[128,2048]{1,0:T(8,128)(2,1)} %collective-permute-done.64.refs_4_.refs_2_, bf16[128,2048]{1,0:T(8,128)(2,1)} %collective-permute-done.65.refs_5_.refs_3_, ...), custom_call_target="tpu_custom_call" | custom-call | flops 1073741824 | bytes 8388608 | tf_op jit(solution)/shard_map/weight_grads/pallas_call | solution.py:403
  626.5 11.8 %weight_grads.7 = bf16[16,1,128,512]{3,2,1,0:T(8,128)(2,1)} custom-call(s32[9]{0:T(128)} %pad_add_fusion.places, bf16[128,2048]{1,0:T(8,128)(2,1)} %copy-done.6, bf16[128,2048]{1,0:T(8,128)(2,1)} %copy-done.15, bf16[128,2048]{1,0:T(8,128)(2,1)} %copy-done.14, bf16[128,2048]{1,0:T(8,128)(2,1)} %copy-done.18, ...), custom_call_target="tpu_custom_call", output_to_operand_aliasing={{}: (18, {})} | custom-call | flops 3221225472 | bytes 8388608 | tf_op jit(solution)/shard_map/weight_grads/pallas_call | solution.py:403
  660.6 16.8 %collective-permute-done.83 = bf16[128,2048]{1,0:T(8,128)(2,1)S(1)} collective-permute-done((bf16[128,2048]{1,0:T(8,128)(2,1)S(1)}, bf16[128,2048]{1,0:T(8,128)(2,1)S(1)}, u32[]{:S(2)}, u32[]{:S(2)}) %collective-permute-start.83) | collective-permute-done | bytes 524320 | tf_op jit(solution)/shard_map/ppermute | solution.py:25
  688.0 11.9 %collective-permute-done.82 = bf16[128,2048]{1,0:T(8,128)(2,1)S(1)} collective-permute-done((bf16[128,2048]{1,0:T(8,128)(2,1)S(1)}, bf16[128,2048]{1,0:T(8,128)(2,1)S(1)}, u32[]{:S(2)}, u32[]{:S(2)}) %collective-permute-start.82) | collective-permute-done | bytes 524320 | tf_op jit(solution)/shard_map/ppermute | solution.py:25
  (366 shorter events, 308.1 us)
Async XLA Ops:
  8.8 57.6 %all-to-all-start = ((bf16[8,144,512]{2,1,0:T(8,128)(2,1)}), bf16[8,144,512]{2,1,0:T(8,128)(2,1)}, u32[]{:S(2)}, u32[]{:S(2)}) async-start(bf16[8,144,512]{2,1,0:T(8,128)(2,1)} %pack_heads.1), calls=%async_computation | async-start | bytes 2359296 | tf_op jit(solution)/shard_map/all_to_all | solution.py:112
  17.7 45.3 %collective-permute-start.6 = (bf16[128,2048]{1,0:T(8,128)(2,1)S(1)}, bf16[128,2048]{1,0:T(8,128)(2,1)S(1)}, u32[]{:S(2)}, u32[]{:S(2)}) collective-permute-start(bf16[128,2048]{1,0:T(8,128)(2,1)S(1)} %get-tuple-element.162.refs_2_.refs_0_), channel_id=1, source_target_pairs={{0,16},{2,18},{4,20},{6,22},{8,24},{10,26},{12,28},{14,30},{16,0},... | collective-permute-start | bytes 1572872 | tf_op jit(solution)/shard_map/ppermute | solution.py:25
  17.8 48.5 %collective-permute-start.4 = (bf16[128,2048]{1,0:T(8,128)(2,1)S(1)}, bf16[128,2048]{1,0:T(8,128)(2,1)S(1)}, u32[]{:S(2)}, u32[]{:S(2)}) collective-permute-start(bf16[128,2048]{1,0:T(8,128)(2,1)S(1)} %get-tuple-element.162.refs_2_.refs_0_), channel_id=1, source_target_pairs={{0,4},{2,6},{4,0},{6,2},{8,12},{10,14},{12,8},{14,10},{16,20},{18,... | collective-permute-start | bytes 1572872 | tf_op jit(solution)/shard_map/ppermute | solution.py:25
  19.8 47.4 %collective-permute-start.2 = (bf16[128,2048]{1,0:T(8,128)(2,1)S(1)}, bf16[128,2048]{1,0:T(8,128)(2,1)S(1)}, u32[]{:S(2)}, u32[]{:S(2)}) collective-permute-start(bf16[128,2048]{1,0:T(8,128)(2,1)S(1)} %get-tuple-element.162.refs_2_.refs_0_), channel_id=1, source_target_pairs={{0,2},{2,0},{4,6},{6,4},{8,10},{10,8},{12,14},{14,12},{16,18},{18,... | collective-permute-start | bytes 1572872 | tf_op jit(solution)/shard_map/ppermute | solution.py:25
  21.2 46.4 %collective-permute-start.1 = (bf16[128,2048]{1,0:T(8,128)(2,1)S(1)}, bf16[128,2048]{1,0:T(8,128)(2,1)S(1)}, u32[]{:S(2)}, u32[]{:S(2)}) collective-permute-start(bf16[128,2048]{1,0:T(8,128)(2,1)S(1)} %get-tuple-element.162.refs_2_.refs_0_), channel_id=1, source_target_pairs={{0,1},{1,0},{2,3},{3,2},{4,5},{5,4},{6,7},{7,6},{8,9},{9,8},{10,11... | collective-permute-start | bytes 1572872 | tf_op jit(solution)/shard_map/ppermute | solution.py:29
  67.2 33.0 %collective-permute-start = (bf16[8,144,512]{2,1,0:T(8,128)(2,1)}, bf16[8,144,512]{2,1,0:T(8,128)(2,1)}, u32[]{:S(2)}, u32[]{:S(2)}) collective-permute-start(bf16[8,144,512]{2,1,0:T(8,128)(2,1)} %all-to-all-done.refs_0_), channel_id=1, source_target_pairs={{0,8},{2,10},{4,12},{6,14},{8,0},{10,2},{12,4},{14,6},{16,24},{18,... | collective-permute-start | bytes 3538952 | tf_op jit(solution)/shard_map/ppermute | solution.py:25
  133.5 103.0 %all-to-all-start.1 = ((bf16[8,3,128,352]{2,3,1,0:T(8,128)(2,1)}), bf16[8,3,128,352]{2,3,1,0:T(8,128)(2,1)S(1)}, u32[]{:S(2)}, u32[]{:S(2)}) async-start(bf16[8,3,128,352]{2,3,1,0:T(8,128)(2,1)} %copy.147), calls=%async_computation.1 | async-start | bytes 4325376 | tf_op jit(solution)/shard_map/all_to_all | solution.py:112
  167.8 40.5 %collective-permute-start.28 = (bf16[128,2048]{1,0:T(8,128)(2,1)}, bf16[128,2048]{1,0:T(8,128)(2,1)}, u32[]{:S(2)}, u32[]{:S(2)}) collective-permute-start(bf16[128,2048]{1,0:T(8,128)(2,1)} %broadcast_select_fusion.refs_18_.refs_0_), channel_id=1, source_target_pairs={{0,16},{2,18},{4,20},{6,22},{8,24},{10,26},{12,28},{14,30},{16,0},... | collective-permute-start | bytes 1572872 | tf_op jit(solution)/shard_map/ppermute | solution.py:25
  236.7 59.1 %collective-permute-start.26 = (bf16[8,3,128,352]{2,3,1,0:T(8,128)(2,1)S(1)}, bf16[8,3,128,352]{2,3,1,0:T(8,128)(2,1)S(1)}, u32[]{:S(2)}, u32[]{:S(2)}) collective-permute-start(bf16[8,3,128,352]{2,3,1,0:T(8,128)(2,1)S(1)} %all-to-all-done.1), channel_id=1, source_target_pairs={{0,8},{2,10},{4,12},{6,14},{8,0},{10,2},{12,4},{14,6},{16,24},{18,... | collective-permute-start | bytes 6488072 | tf_op jit(solution)/shard_map/ppermute | solution.py:25
  249.1 45.5 %collective-permute-start.37 = (bf16[128,2048]{1,0:T(8,128)(2,1)S(1)}, bf16[128,2048]{1,0:T(8,128)(2,1)S(1)}, u32[]{:S(2)}, u32[]{:S(2)}) collective-permute-start(bf16[128,2048]{1,0:T(8,128)(2,1)S(1)} %multiply_convert_fusion.refs_2_.refs_0_), channel_id=1, source_target_pairs={{0,16},{2,18},{4,20},{6,22},{8,24},{10,26},{12,28},{14,30},{16,0},... | collective-permute-start | bytes 1572872 | tf_op jit(solution)/shard_map/ppermute | solution.py:25
  249.9 47.8 %collective-permute-start.35 = (bf16[128,2048]{1,0:T(8,128)(2,1)S(1)}, bf16[128,2048]{1,0:T(8,128)(2,1)S(1)}, u32[]{:S(2)}, u32[]{:S(2)}) collective-permute-start(bf16[128,2048]{1,0:T(8,128)(2,1)S(1)} %multiply_convert_fusion.refs_2_.refs_0_), channel_id=1, source_target_pairs={{0,4},{2,6},{4,0},{6,2},{8,12},{10,14},{12,8},{14,10},{16,20},{18,... | collective-permute-start | bytes 1572872 | tf_op jit(solution)/shard_map/ppermute | solution.py:25
  251.0 46.8 %collective-permute-start.33 = (bf16[128,2048]{1,0:T(8,128)(2,1)S(1)}, bf16[128,2048]{1,0:T(8,128)(2,1)}, u32[]{:S(2)}, u32[]{:S(2)}) collective-permute-start(bf16[128,2048]{1,0:T(8,128)(2,1)S(1)} %multiply_convert_fusion.refs_2_.refs_0_), channel_id=1, source_target_pairs={{0,2},{2,0},{4,6},{6,4},{8,10},{10,8},{12,14},{14,12},{16,18},{18,... | collective-permute-start | bytes 1572872 | tf_op jit(solution)/shard_map/ppermute | solution.py:25
  252.4 45.9 %collective-permute-start.32 = (bf16[128,2048]{1,0:T(8,128)(2,1)S(1)}, bf16[128,2048]{1,0:T(8,128)(2,1)S(1)}, u32[]{:S(2)}, u32[]{:S(2)}) collective-permute-start(bf16[128,2048]{1,0:T(8,128)(2,1)S(1)} %multiply_convert_fusion.refs_2_.refs_0_), channel_id=1, source_target_pairs={{0,1},{1,0},{2,3},{3,2},{4,5},{5,4},{6,7},{7,6},{8,9},{9,8},{10,11... | collective-permute-start | bytes 1572872 | tf_op jit(solution)/shard_map/ppermute | solution.py:29
  392.7 47.5 %collective-permute-start.57 = (bf16[256,2048]{1,0:T(8,128)(2,1)}, bf16[256,2048]{1,0:T(8,128)(2,1)S(1)}, u32[]{:S(2)}, u32[]{:S(2)}) collective-permute-start(bf16[256,2048]{1,0:T(8,128)(2,1)} %get-tuple-element.168), channel_id=1, source_target_pairs={{0,2},{2,0},{4,6},{6,4},{8,10},{10,8},{12,14},{14,12},{16,18},{18,... | collective-permute-start | bytes 3145736 | tf_op jit(solution)/shard_map/ppermute | solution.py:25
  394.2 47.1 %collective-permute-start.56 = (bf16[256,2048]{1,0:T(8,128)(2,1)}, bf16[256,2048]{1,0:T(8,128)(2,1)}, u32[]{:S(2)}, u32[]{:S(2)}) collective-permute-start(bf16[256,2048]{1,0:T(8,128)(2,1)} %get-tuple-element.170), channel_id=1, source_target_pairs={{0,4},{2,6},{4,0},{6,2},{8,12},{10,14},{12,8},{14,10},{16,20},{18,... | collective-permute-start | bytes 3145736 | tf_op jit(solution)/shard_map/ppermute | solution.py:25
  476.9 47.7 %collective-permute-start.62 = (bf16[256,2048]{1,0:T(8,128)(2,1)}, bf16[256,2048]{1,0:T(8,128)(2,1)}, u32[]{:S(2)}, u32[]{:S(2)}) collective-permute-start(bf16[256,2048]{1,0:T(8,128)(2,1)} %add_convert_fusion), channel_id=1, source_target_pairs={{0,16},{2,18},{4,20},{6,22},{8,24},{10,26},{12,28},{14,30},{16,0},... | collective-permute-start | bytes 3145736 | tf_op jit(solution)/shard_map/ppermute | solution.py:25
  486.9 96.4 %all-to-all-start.2 = ((bf16[2,8,3,128,352]{3,4,2,1,0:T(8,128)(2,1)}), bf16[2,8,3,128,352]{3,4,2,1,0:T(8,128)(2,1)}, u32[]{:S(2)}, u32[]{:S(2)}) async-start(bf16[2,8,3,128,352]{3,4,2,1,0:T(8,128)(2,1)} %copy.155), calls=%async_computation.2 | async-start | bytes 8650752 | tf_op jit(solution)/shard_map/all_to_all | solution.py:128
  529.1 32.5 %collective-permute-start.66 = (bf16[128,2048]{1,0:T(8,128)(2,1)S(1)}, bf16[128,2048]{1,0:T(8,128)(2,1)S(1)}, u32[]{:S(2)}, u32[]{:S(2)}) collective-permute-start(bf16[128,2048]{1,0:T(8,128)(2,1)S(1)} %fusion.40.refs_2_.refs_0_), channel_id=1, source_target_pairs={{0,4},{2,6},{4,0},{6,2},{8,12},{10,14},{12,8},{14,10},{16,20},{18,... | collective-permute-start | bytes 1572872 | tf_op jit(solution)/shard_map/ppermute | solution.py:25
  588.3 55.7 %all-to-all-start.4 = ((bf16[8,3,128,352]{2,3,1,0:T(8,128)(2,1)}), bf16[8,3,128,352]{2,3,1,0:T(8,128)(2,1)}, u32[]{:S(2)}, u32[]{:S(2)}) async-start(bf16[8,3,128,352]{2,3,1,0:T(8,128)(2,1)} %reduce_sum.91), calls=%async_computation.4 | async-start | bytes 4325376 | tf_op jit(solution)/shard_map/all_to_all | solution.py:112
  616.8 35.3 %collective-permute-start.78 = (bf16[8,128,2048]{2,1,0:T(8,128)(2,1)}, bf16[8,128,2048]{2,1,0:T(8,128)(2,1)}, u32[]{:S(2)}, u32[]{:S(2)}) collective-permute-start(bf16[8,128,2048]{2,1,0:T(8,128)(2,1)} %get-tuple-element.93), channel_id=1, source_target_pairs={{0,1},{1,0},{2,3},{3,2},{4,5},{5,4},{6,7},{7,6},{8,9},{9,8},{10,11... | collective-permute-start | bytes 12582920 | tf_op jit(solution)/shard_map/ppermute | solution.py:29
  644.0 72.2 %all-to-all-start.3 = ((bf16[16,128,512]{2,1,0:T(8,128)(2,1)}), bf16[16,128,512]{2,1,0:T(8,128)(2,1)}, u32[]{:S(2)}, u32[]{:S(2)}) async-start(bf16[16,128,512]{2,1,0:T(8,128)(2,1)} %bitcast.117), calls=%async_computation.3 | async-start | bytes 4194304 | tf_op jit(solution)/shard_map/all_to_all | solution.py:736
  660.1 39.8 %collective-permute-start.82 = (bf16[128,2048]{1,0:T(8,128)(2,1)S(1)}, bf16[128,2048]{1,0:T(8,128)(2,1)S(1)}, u32[]{:S(2)}, u32[]{:S(2)}) collective-permute-start(bf16[128,2048]{1,0:T(8,128)(2,1)S(1)} %get-tuple-element.101), channel_id=1, source_target_pairs={{0,2},{2,0},{4,6},{6,4},{8,10},{10,8},{12,14},{14,12},{16,18},{18,... | collective-permute-start | bytes 1572872 | tf_op jit(solution)/shard_map/ppermute | solution.py:25
  679.6 53.6 %collective-permute-start.81 = (bf16[128,2048]{1,0:T(8,128)(2,1)}, bf16[128,2048]{1,0:T(8,128)(2,1)}, u32[]{:S(2)}, u32[]{:S(2)}) collective-permute-start(bf16[128,2048]{1,0:T(8,128)(2,1)} %get-tuple-element.99), channel_id=1, source_target_pairs={{0,4},{2,6},{4,0},{6,2},{8,12},{10,14},{12,8},{14,10},{16,20},{18,... | collective-permute-start | bytes 1572872 | tf_op jit(solution)/shard_map/ppermute | solution.py:25
  687.0 46.2 %collective-permute-start.80 = (bf16[128,2048]{1,0:T(8,128)(2,1)}, bf16[128,2048]{1,0:T(8,128)(2,1)}, u32[]{:S(2)}, u32[]{:S(2)}) collective-permute-start(bf16[128,2048]{1,0:T(8,128)(2,1)} %add_convert_fusion.12), channel_id=1, source_target_pairs={{0,2},{2,0},{4,6},{6,4},{8,10},{10,8},{12,14},{14,12},{16,18},{18,... | collective-permute-start | bytes 1572872 | tf_op jit(solution)/shard_map/ppermute | solution.py:25
  (121 other events, 2047.0 us)
